TPU v7x, 32 devices: a whole 2x2x4 slice. The times are simulated.
32 devices in a mesh: dp: 8 (over z, y), fsdp: 4 (over x, core).
Axes of the slice: x: 2, y: 2, z: 4, core: 2. Of those that a mesh axis runs over, the one named last changes fastest.
Arguments:
- tokens: bfloat16 [96, 256, 768], P(('dp', 'fsdp')), may hold values from -6 to 6
- qkv_weight: bfloat16 [768, 2304], P('dp', 'fsdp'), may hold values from -0.21875 to 0.21875
- out_weight: bfloat16 [768, 768], P('dp', 'fsdp'), may hold values from -0.875 to 0.875
- up_weight: bfloat16 [768, 3072], P('dp', 'fsdp'), may hold values from -0.21875 to 0.21875
- up_bias: bfloat16 [3072], P(('dp', 'fsdp')), may hold values from -1.75 to 1.75
- down_weight: bfloat16 [3072, 768], P('dp', 'fsdp'), may hold values from -0.109375 to 0.109375
- vectors: bfloat16 [8, 768], P('fsdp', 'dp'), may hold values from -1.2 to 2.2
- lengths: int32 [96], P(('dp', 'fsdp')), may hold values from 32 to 256, as said below
- exit_depth: int32 [96], P(('dp', 'fsdp')), may hold values from 0 to 1
- prefix_widths: int32 [5], replicated, may hold values from 64 to 768, as said below
- cotangent: bfloat16 [96, 256, 768], P(('dp', 'fsdp')), may hold values from -12 to 12
Outputs:
- layer_out: bfloat16 [96, 256, 768], P(('dp', 'fsdp'))
- pooled: float32 [96, 5, 768], P(('dp', 'fsdp'))
- grad_tokens: bfloat16 [96, 256, 768], P(('dp', 'fsdp'))
- grad_qkv_weight: float32 [768, 2304], P('dp', 'fsdp')
- grad_out_weight: float32 [768, 768], P('dp', 'fsdp')
- grad_up_weight: float32 [768, 3072], P('dp', 'fsdp')
- grad_up_bias: float32 [3072], P(('dp', 'fsdp'))
- grad_down_weight: float32 [3072, 768], P('dp', 'fsdp')
- grad_vectors: float32 [8, 768], P('fsdp', 'dp')
Inputs may be any that keep to these rules, and one draw needn't show every extreme that they name: `lengths`: at least one sentence has all 256 slots valid and one has 32. `prefix_widths`: an order of 768, 512, 256, 128, 64.
All inputs are finite; a program needn't handle non-finite values.
Results may differ from a plain program's by a relative error of at most 0.019.
Values may be sent and summed in bfloat16 or wider, within the bound.
No kernel may reach another device: no remote copies, remote signals or barrier semaphores. Data moves between devices by JAX's collectives and lax.ppermute only.
A program may use at most 192 MiB of HBM per device.

v0:
```python
from functools import partial

import jax
import jax.numpy as jnp
from jax import lax
from jax.sharding import PartitionSpec as P

HEAD_DIM = 64


EPS = 1e-05


def norm_keep(hidden, norm_gain, norm_shift):
    row_mean = jnp.mean(hidden, axis=-1, keepdims=True)
    centered = hidden - row_mean
    spread = jnp.mean(centered * centered, axis=-1, keepdims=True)
    factor = lax.rsqrt(spread + EPS)
    normed = centered * factor
    return (normed * norm_gain + norm_shift, normed, factor)


def norm_back(grad_in, normed, factor, norm_gain):
    d_gain = jnp.sum(grad_in * normed, axis=0)
    d_shift = jnp.sum(grad_in, axis=0)
    scaled = grad_in * norm_gain
    d_hidden = factor * (
        scaled
        - jnp.mean(scaled, axis=-1, keepdims=True)
        - normed * jnp.mean(scaled * normed, axis=-1, keepdims=True)
    )
    return (d_hidden, d_gain, d_shift)


def masked_scores(queries, key_rows, key_keep):
    scores = jnp.einsum(
        "sqhd,skhd->shqk", queries, key_rows, preferred_element_type=jnp.float32
    ) * HEAD_DIM ** (-0.5)
    return jnp.where(key_keep, scores, -1000000000.0)


def local(
    tokens,
    qkv_weight,
    out_weight,
    up_weight,
    up_bias,
    down_weight,
    vectors,
    lengths,
    exit_depth,
    prefix_widths,
    cotangent,
):
    sent_count, seq_len, model_width = tokens.shape
    row_count = sent_count * seq_len
    head_count = model_width // HEAD_DIM
    key_scale = HEAD_DIM ** (-0.5)
    qkv_part, out_part, up_part, bias_part, down_part, vec_part = (
        lax.all_gather(qkv_weight, "fsdp", axis=1, tiled=True),
        lax.all_gather(out_weight, "fsdp", axis=1, tiled=True),
        lax.all_gather(up_weight, "fsdp", axis=1, tiled=True),
        lax.all_gather(up_bias, "fsdp", axis=0, tiled=True),
        lax.all_gather(down_weight, "fsdp", axis=1, tiled=True),
        lax.all_gather(vectors, "fsdp", axis=0, tiled=True),
    )
    w_qkv, w_out, w_up, b_up, w_down, vec_full = (
        lax.all_gather(qkv_part, "dp", axis=0, tiled=True),
        lax.all_gather(out_part, "dp", axis=0, tiled=True),
        lax.all_gather(up_part, "dp", axis=0, tiled=True),
        lax.all_gather(bias_part, "dp", axis=0, tiled=True),
        lax.all_gather(down_part, "dp", axis=0, tiled=True),
        lax.all_gather(vec_part, "dp", axis=1, tiled=True),
    )
    vec_f = vec_full.astype(jnp.float32)
    inputs = tokens.reshape(row_count, model_width)
    qkv_bias = jnp.concatenate([vec_f[0], jnp.zeros_like(vec_f[0]), vec_f[1]])
    joined_qkv = (jnp.dot(inputs, w_qkv, preferred_element_type=jnp.float32) + qkv_bias).astype(
        jnp.bfloat16
    )
    split_parts = joined_qkv.reshape(sent_count, seq_len, 3, head_count, HEAD_DIM)
    queries = split_parts[:, :, 0]
    key_rows = split_parts[:, :, 1]
    values = split_parts[:, :, 2]
    positions = lax.broadcasted_iota(jnp.int32, (sent_count, seq_len), 1)
    valid_rows = positions < lengths[:, None]
    key_keep = valid_rows[:, None, None, :]
    scores = masked_scores(queries, key_rows, key_keep)
    row_top = jnp.max(scores, axis=-1, keepdims=True)
    exponent = jnp.exp(scores - row_top)
    row_total = jnp.sum(exponent, axis=-1, keepdims=True)
    prob_low = (exponent / row_total).astype(jnp.bfloat16)
    log_total = row_top + jnp.log(row_total)
    attended = jnp.einsum("shqk,skhd->sqhd", prob_low, values, preferred_element_type=jnp.float32)
    attended = attended.reshape(row_count, model_width).astype(jnp.bfloat16)
    first_sum = inputs.astype(jnp.float32) + (
        jnp.dot(attended, w_out, preferred_element_type=jnp.float32) + vec_f[2]
    )
    first_out, normed_first, factor_first = norm_keep(first_sum, vec_f[3], vec_f[4])
    first_norm = first_out.astype(jnp.bfloat16)
    pre_act = jnp.dot(first_norm, w_up, preferred_element_type=jnp.float32) + b_up.astype(
        jnp.float32
    )
    activated, gelu_pull = jax.vjp(partial(jax.nn.gelu, approximate=False), pre_act)
    activated = activated.astype(jnp.bfloat16)
    second_sum = first_norm.astype(jnp.float32) + (
        jnp.dot(activated, w_down, preferred_element_type=jnp.float32) + vec_f[5]
    )
    result, normed_second, factor_second = norm_keep(second_sum, vec_f[6], vec_f[7])
    result = result.reshape(sent_count, seq_len, model_width)
    layer_out = result.astype(jnp.bfloat16)
    valid_mask = valid_rows.astype(jnp.float32)
    source = jnp.where((exit_depth == 1)[:, None, None], result, tokens.astype(jnp.float32))
    pooled_mean = (
        jnp.sum(valid_mask[:, :, None] * source, axis=1) / lengths.astype(jnp.float32)[:, None]
    )
    columns = lax.broadcasted_iota(jnp.int32, (prefix_widths.shape[0], model_width), 1)
    prefix = (columns < prefix_widths[:, None]).astype(jnp.float32)
    pooled = pooled_mean[:, None, :] * prefix[None, :, :]
    w_qkv_part, w_out_part, w_up_part, w_down_part = (
        lax.all_gather(qkv_weight, "fsdp", axis=1, tiled=True),
        lax.all_gather(out_weight, "fsdp", axis=1, tiled=True),
        lax.all_gather(up_weight, "fsdp", axis=1, tiled=True),
        lax.all_gather(down_weight, "fsdp", axis=1, tiled=True),
    )
    w_qkv, w_out, w_up, w_down = (
        lax.all_gather(w_qkv_part, "dp", axis=0, tiled=True),
        lax.all_gather(w_out_part, "dp", axis=0, tiled=True),
        lax.all_gather(w_up_part, "dp", axis=0, tiled=True),
        lax.all_gather(w_down_part, "dp", axis=0, tiled=True),
    )
    grad_out = cotangent.reshape(row_count, model_width).astype(jnp.float32)
    d_second, d_gain_second, d_shift_second = norm_back(
        grad_out, normed_second, factor_second, vec_f[6]
    )
    d_down = d_second.astype(jnp.bfloat16)
    grad_down = jnp.dot(activated.T, d_down, preferred_element_type=jnp.float32)
    bias_down = jnp.sum(d_down.astype(jnp.float32), axis=0)
    d_act = jnp.dot(d_down, w_down.T, preferred_element_type=jnp.float32)
    d_pre = gelu_pull(d_act)[0].astype(jnp.bfloat16)
    grad_up = jnp.dot(first_norm.T, d_pre, preferred_element_type=jnp.float32)
    grad_bias_up = jnp.sum(d_pre.astype(jnp.float32), axis=0)
    d_first = jnp.dot(d_pre, w_up.T, preferred_element_type=jnp.float32) + d_second
    d_resid, d_gain_first, d_shift_first = norm_back(d_first, normed_first, factor_first, vec_f[3])
    d_attn = d_resid.astype(jnp.bfloat16)
    grad_out_proj = jnp.dot(attended.T, d_attn, preferred_element_type=jnp.float32)
    bias_out = jnp.sum(d_attn.astype(jnp.float32), axis=0)
    d_att = jnp.dot(d_attn, w_out.T, preferred_element_type=jnp.float32).astype(jnp.bfloat16)
    d_att = d_att.reshape(sent_count, seq_len, head_count, HEAD_DIM)
    scores = masked_scores(queries, key_rows, key_keep)
    prob_full = jnp.exp(scores - log_total)
    d_values = jnp.einsum(
        "shqk,sqhd->skhd", prob_full.astype(jnp.bfloat16), d_att, preferred_element_type=jnp.float32
    )
    d_probs = jnp.einsum("sqhd,skhd->shqk", d_att, values, preferred_element_type=jnp.float32)
    row_dot = jnp.sum(d_probs * prob_full, axis=-1, keepdims=True)
    d_scores = (prob_full * (d_probs - row_dot)).astype(jnp.bfloat16)
    d_queries = (
        jnp.einsum("shqk,skhd->sqhd", d_scores, key_rows, preferred_element_type=jnp.float32)
        * key_scale
    )
    d_keys = (
        jnp.einsum("shqk,sqhd->skhd", d_scores, queries, preferred_element_type=jnp.float32)
        * key_scale
    )
    d_joined = (
        jnp.stack([d_queries, d_keys, d_values], axis=2)
        .reshape(row_count, 3 * model_width)
        .astype(jnp.bfloat16)
    )
    grad_qkv = jnp.dot(inputs.T, d_joined, preferred_element_type=jnp.float32)
    bias_sums = jnp.sum(d_joined.astype(jnp.float32), axis=0)
    d_inputs = jnp.dot(d_joined, w_qkv.T, preferred_element_type=jnp.float32) + d_resid
    grad_tokens = d_inputs.astype(jnp.bfloat16).reshape(sent_count, seq_len, model_width)
    grad_vec = jnp.stack(
        [
            bias_sums[:model_width],
            bias_sums[2 * model_width :],
            bias_out,
            d_gain_first,
            d_shift_first,
            bias_down,
            d_gain_second,
            d_shift_second,
        ]
    )
    sum_qkv, sum_out, sum_up, sum_bias, sum_down, sum_vec = (
        lax.psum_scatter(
            grad_qkv.astype(jnp.bfloat16), "dp", scatter_dimension=0, tiled=True
        ).astype(jnp.float32),
        lax.psum_scatter(
            grad_out_proj.astype(jnp.bfloat16), "dp", scatter_dimension=0, tiled=True
        ).astype(jnp.float32),
        lax.psum_scatter(
            grad_up.astype(jnp.bfloat16), "dp", scatter_dimension=0, tiled=True
        ).astype(jnp.float32),
        lax.psum_scatter(
            grad_bias_up.astype(jnp.bfloat16), "dp", scatter_dimension=0, tiled=True
        ).astype(jnp.float32),
        lax.psum_scatter(
            grad_down.astype(jnp.bfloat16), "dp", scatter_dimension=0, tiled=True
        ).astype(jnp.float32),
        lax.psum_scatter(
            grad_vec.astype(jnp.bfloat16), "dp", scatter_dimension=1, tiled=True
        ).astype(jnp.float32),
    )
    own_qkv, own_out, own_up, own_bias, own_down, own_vec = (
        lax.psum_scatter(
            sum_qkv.astype(jnp.bfloat16), "fsdp", scatter_dimension=1, tiled=True
        ).astype(jnp.float32),
        lax.psum_scatter(
            sum_out.astype(jnp.bfloat16), "fsdp", scatter_dimension=1, tiled=True
        ).astype(jnp.float32),
        lax.psum_scatter(
            sum_up.astype(jnp.bfloat16), "fsdp", scatter_dimension=1, tiled=True
        ).astype(jnp.float32),
        lax.psum_scatter(
            sum_bias.astype(jnp.bfloat16), "fsdp", scatter_dimension=0, tiled=True
        ).astype(jnp.float32),
        lax.psum_scatter(
            sum_down.astype(jnp.bfloat16), "fsdp", scatter_dimension=1, tiled=True
        ).astype(jnp.float32),
        lax.psum_scatter(
            sum_vec.astype(jnp.bfloat16), "fsdp", scatter_dimension=0, tiled=True
        ).astype(jnp.float32),
    )
    return (layer_out, pooled, grad_tokens, own_qkv, own_out, own_up, own_bias, own_down, own_vec)


def solution(mesh):
    placed = (
        P(("dp", "fsdp"), None, None),
        P("dp", "fsdp"),
        P("dp", "fsdp"),
        P("dp", "fsdp"),
        P(("dp", "fsdp")),
        P("dp", "fsdp"),
        P("fsdp", "dp"),
        P(("dp", "fsdp")),
        P(("dp", "fsdp")),
        P(),
        P(("dp", "fsdp"), None, None),
    )
    return jax.shard_map(
        local,
        mesh=mesh,
        in_specs=placed,
        out_specs=(
            P(("dp", "fsdp"), None, None),
            P(("dp", "fsdp"), None, None),
            P(("dp", "fsdp"), None, None),
            P("dp", "fsdp"),
            P("dp", "fsdp"),
            P("dp", "fsdp"),
            P(("dp", "fsdp")),
            P("dp", "fsdp"),
            P("fsdp", "dp"),
        ),
        check_vma=False,
    )
```

profile of v0, /device:TPU:0, one launch (start us, length us, event | category | flops | bytes accessed | tf_op | source)
XLA Modules:
  0.0 849.5 jit_solution(5933173163193667052)
XLA Ops:
  7.3 8.8 %all-gather = bf16[4,576,96]{1,2,0:T(8,128)(2,1)S(1)} all-gather(bf16[1,576,96]{1,2,0:T(8,128)(2,1)} %bitcast.132), channel_id=1, replica_groups=mesh['dp'=8,'fsdp'=4] {'fsdp'}, dimensions={0}, use_global_device_ids=true | all-gather | bytes 552960 | tf_op jit(solution)/shard_map/all_gather | solution.py:60
  18.5 5.6 all_gather.48
  25.0 8.1 all_gather.50
  33.2 8.1 all_gather.54
  41.4 5.0 all-gather.1
  46.4 26.8 %all-gather.2 = bf16[8,96,8]{1,2,0:T(8,128)(2,1)S(1)} all-gather(bf16[1,96,8]{1,2,0:T(8,128)(2,1)S(1)} %bitcast.138), channel_id=1, replica_groups=mesh['dp'=8,'fsdp'=4] {'dp'}, dimensions={0}, use_global_device_ids=true | all-gather | bytes 13824 | tf_op jit(solution)/shard_map/all_gather | solution.py:73
  75.4 6.0 all-reduce
  81.5 26.2 %all-gather.3 = bf16[8,1,384]{2,1,0:T(2,128)(2,1)S(1)} all-gather(bf16[1,1,384]{2,1,0:T(2,128)(2,1)S(1)} %reshape.195), channel_id=1, replica_groups=mesh['dp'=8,'fsdp'=4] {'dp'}, dimensions={0}, use_global_device_ids=true | all-gather | bytes 6912 | tf_op jit(solution)/shard_map/all_gather | solution.py:71
  109.9 6.4 add_convert_fusion.1
  116.2 11.6 %reshape.212 = bf16[3,256,3,12,64]{4,3,2,1,0:T(8,128)(2,1)} reshape(bf16[768,2304]{1,0:T(8,128)(2,1)} %add_convert_fusion.1) | data formatting | bytes 7077888 | tf_op jit(solution)/shard_map/reshape | solution.py:81
  127.9 6.9 fusion.50
  134.8 3.8 copy.119
  138.6 4.1 copy.118
  142.7 5.0 copy.117
  147.7 2.4 fusion.13
  150.2 2.4 fusion.6
  153.9 2.9 fusion.25
  159.2 3.3 fusion.53
  164.4 42.9 %all-gather.13.cloned.1.call-done = bf16[768,3072]{1,0:T(8,128)(2,1)} async-done(((bf16[96,3072]{1,0:T(8,128)(2,1)}), bf16[768,3072]{1,0:T(8,128)(2,1)}) %all-gather.13.cloned.1.call-update) | async-done | bytes 4718608 | tf_op jit(solution)/shard_map/all_gather | solution.py:70
  207.3 28.5 %multiply_convert_fusion.1 = (bf16[768,3072]{1,0:T(8,128)(2,1)}, f32[768,3072]{1,0:T(8,128)}, f32[768,3072]{1,0:T(8,128)}) fusion(f32[3072]{0:T(1024)} %bitcast.136, bf16[768,3072]{1,0:T(8,128)(2,1)} %all-gather.13.cloned.1.call-done, f32[768,768]{1,0:T(8,128)S(1)} %get-tuple-element.91, f32[768]{0:T(1024)} %get-tuple-element.63, ...), kind=kOutput, calls=%fused_computation.6 | convolution fusion | flops 3782541312 | bytes 30695424 | tf_op jit(solution)/shard_map/dot_general | solution.py:101
  235.8 52.6 %all-gather.15.cloned.1.call-done = bf16[3072,768]{0,1:T(8,128)(2,1)} async-done(((bf16[384,768]{0,1:T(8,128)(2,1)}), bf16[3072,768]{0,1:T(8,128)(2,1)}) %all-gather.15.cloned.1.call-update) | async-done | bytes 4718608 | tf_op jit(solution)/shard_map/all_gather | solution.py:72
  288.4 7.6 fusion.54
  299.7 13.7 %fusion.55 = (bf16[3072]{0:T(1024)(128)(2,1)}, bf16[768,3072]{1,0:T(8,128)(2,1)}) fusion(f32[768,3072]{1,0:T(8,128)} %get-tuple-element.77, bf16[3072,768]{0,1:T(8,128)(2,1)S(1)} %bitcast.143, f32[768,768]{1,0:T(8,128)S(1)} %get-tuple-element.71, f32[768,3072]{1,0:T(8,128)} %get-tuple-element.92, f32[3072]{0:T(1024)S(1)} %bitcast.137), kind=kOutput, calls=%fused_computation.119 | convolution fusion | flops 3662214144 | bytes 30689280 | tf_op jit(solution)/shard_map/dot_general | solution.py:139
  313.4 7.7 multiply_reduce_fusion.1
  323.9 2.2 convolution_convert_fusion.3
  326.1 4.1 convolution_convert_fusion.4
  330.2 4.7 reshape.213
  334.9 4.6 copy.93
  339.5 7.9 multiply_reduce_fusion
  347.4 6.8 multiply_convert_fusion
  357.1 2.6 fusion.21
  361.0 3.4 copy.98
  367.3 4.3 fusion.12
  371.6 5.8 copy.105
  377.7 9.2 %convolution_convert_fusion.1 = bf16[3072,768]{1,0:T(8,128)(2,1)} fusion(bf16[768,3072]{1,0:T(8,128)(2,1)} %get-tuple-element.76, f32[768,768]{1,0:T(8,128)} %copy-done.12), kind=kOutput, calls=%fused_computation.28 | convolution fusion | flops 3626827776 | bytes 11796480 | tf_op jit(solution)/shard_map/dot_general | solution.py:137
  387.5 9.5 %convolution_convert_fusion.2 = bf16[768,3072]{1,0:T(8,128)(2,1)} fusion(bf16[768,3072]{1,0:T(8,128)(2,1)} %get-tuple-element.99, f32[768,768]{1,0:T(8,128)} %copy-done.6, f32[768]{0:T(1024)S(1)} %copy-done.30, f32[768]{0:T(1024)S(1)} %get-tuple-element.64, f32[768]{0:T(1024)S(1)} %copy-done.25, f32[768]{0:T(1024)S(1)} %broadcast_multiply_fusion.6), kind=kOutput, calls=%fused_computation.29 | convolution fusion | flops 3629187072 | bytes 11808768 | tf_op jit(solution)/shard_map/dot_general | solution.py:141
  409.8 73.6 %reduce-scatter.28.cloned.1.call-done = bf16[96,2304]{1,0:T(8,128)(2,1)} async-done(((bf16[768,2304]{1,0:T(8,128)(2,1)}), bf16[96,2304]{1,0:T(8,128)(2,1)}) %reduce-scatter.28.cloned.1.call-update) | async-done | bytes 442384
  485.6 96.3 %reduce-scatter.26.cloned.1.call-done = bf16[384,768]{1,0:T(8,128)(2,1)} async-done(((bf16[3072,768]{1,0:T(8,128)(2,1)}), bf16[384,768]{1,0:T(8,128)(2,1)}) %reduce-scatter.26.cloned.1.call-update) | async-done | bytes 589840 | tf_op jit(solution)/shard_map/reduce_scatter | solution.py:200
  581.9 2.1 copy.109
  591.2 89.9 %reduce-scatter.22.cloned.1.call-done = bf16[96,3072]{1,0:T(8,128)(2,1)} async-done(((bf16[768,3072]{1,0:T(8,128)(2,1)}), bf16[96,3072]{1,0:T(8,128)(2,1)}) %reduce-scatter.22.cloned.1.call-update) | async-done | bytes 589840 | tf_op jit(solution)/shard_map/reduce_scatter | solution.py:194
  683.6 20.7 %all-reduce.1 = bf16[3072]{0:T(1024)(128)(2,1)S(1)} all-reduce(bf16[3072]{0:T(1024)(128)(2,1)S(1)} %copy-done.29), channel_id=8, replica_groups=mesh['dp'=8,'fsdp'=4] {'dp'}, use_global_device_ids=true, to_apply=%region_19.20.clone | all-reduce | flops 3072 | bytes 12288
  704.4 7.7 add_convert_fusion.2
  712.1 33.6 %reduce-scatter.34.cloned.1.call-done = bf16[96,8]{1,0:T(8,128)(2,1)} async-done(((bf16[768,8]{1,0:T(8,128)(2,1)}), bf16[96,8]{1,0:T(8,128)(2,1)}) %reduce-scatter.34.cloned.1.call-update) | async-done | bytes 1552
  746.5 5.7 all-reduce.4
  753.3 14.1 %reduce-scatter.30.cloned.1.call-done = bf16[192,96]{1,0:T(8,128)(2,1)} async-done(((bf16[768,96]{1,0:T(8,128)(2,1)}), bf16[192,96]{1,0:T(8,128)(2,1)}) %reduce-scatter.30.cloned.1.call-update) | async-done | bytes 36880
  768.9 23.0 %reduce-scatter.18.cloned.1.call-done = bf16[96,576]{0,1:T(8,128)(2,1)} async-done(((bf16[96,2304]{0,1:T(8,128)(2,1)}), bf16[96,576]{0,1:T(8,128)(2,1)}) %reduce-scatter.18.cloned.1.call-update) | async-done | bytes 110608 | tf_op jit(solution)/shard_map/reduce_scatter | solution.py:208
  793.7 22.7 %reduce-scatter.32.cloned.1.call-done = bf16[192,384]{1,0:T(8,128)(2,1)} async-done(((bf16[768,384]{1,0:T(8,128)(2,1)}), bf16[192,384]{1,0:T(8,128)(2,1)}) %reduce-scatter.32.cloned.1.call-update) | async-done | bytes 147472
  818.3 22.7 %reduce-scatter.24.cloned.1.call-done = bf16[96,768]{1,0:T(8,128)(2,1)} async-done(((bf16[96,3072]{1,0:T(8,128)(2,1)}), bf16[96,768]{1,0:T(8,128)(2,1)}) %reduce-scatter.24.cloned.1.call-update) | async-done | bytes 147472 | tf_op jit(solution)/shard_map/reduce_scatter | solution.py:214
  (186 shorter events, 58.4 us)
Async XLA Ops:
  7.2 66.7 %copy-start.32 = (u32[32]{0:T(128)S(1)}, u32[32]{0:T(128)}, u32[]{:S(2)}) copy-start(u32[32]{0:T(128)} %constant.98) | copy-start | bytes 388
  7.2 17.8 %copy-start.22 = (bf16[96,768]{1,0:T(8,128)(2,1)S(1)}, bf16[96,768]{1,0:T(8,128)(2,1)}, u32[]{:S(2)}) copy-start(bf16[96,768]{1,0:T(8,128)(2,1)} %param.14) | copy-start | bytes 442372
  7.2 26.0 %copy-start.23 = (bf16[384,192]{0,1:T(8,128)(2,1)S(1)}, bf16[384,192]{0,1:T(8,128)(2,1)}, u32[]{:S(2)}) copy-start(bf16[384,192]{0,1:T(8,128)(2,1)} %param.16) | copy-start | bytes 442372
  7.2 34.2 %copy-start.33 = (bf16[2,96]{1,0:T(2,128)(2,1)S(1)}, bf16[2,96]{1,0:T(2,128)(2,1)}, u32[]{:S(2)}) copy-start(bf16[2,96]{1,0:T(2,128)(2,1)} %param.17) | copy-start | bytes 1156
  7.2 67.9 %copy-start.35 = (bf16[96]{0:T(256)(128)(2,1)S(1)}, bf16[96]{0:T(256)(128)(2,1)}, u32[]{:S(2)}) copy-start(bf16[96]{0:T(256)(128)(2,1)} %param.15) | copy-start | bytes 580
  7.2 101.0 %copy-start.34 = (s32[3]{0:T(128)S(1)}, s32[3]{0:T(128)}, u32[]{:S(2)}) copy-start(s32[3]{0:T(128)} %param.18) | copy-start | bytes 40
  7.2 101.7 %copy-start.1 = (bf16[3,256,768]{2,1,0:T(8,128)(2,1)S(1)}, bf16[3,256,768]{2,1,0:T(8,128)(2,1)}, u32[]{:S(2)}) copy-start(bf16[3,256,768]{2,1,0:T(8,128)(2,1)} %param.21) | copy-start | bytes 3538948
  7.3 102.6 %all-gather.9.cloned.1.call-start = ((), (), s32[]{:S(2)}) async-start(), calls=%async_computation.9 | async-start | bytes 3981312 | tf_op jit(solution)/shard_map/all_gather | solution.py:68
  16.1 93.8 %copy-start.13 = (bf16[3,256,768]{2,1,0:T(8,128)(2,1)S(1)}, bf16[3,256,768]{2,1,0:T(8,128)(2,1)}, u32[]{:S(2)}) copy-start(bf16[3,256,768]{2,1,0:T(8,128)(2,1)} %param.11) | copy-start | bytes 3538948
  17.5 141.6 %all-gather.11.cloned.1.call-start = ((), (), s32[]{:S(2)}) async-start(), calls=%async_computation.10 | async-start | bytes 1327104 | tf_op jit(solution)/shard_map/all_gather | solution.py:69
  24.9 182.3 %all-gather.13.cloned.1.call-start = ((), (), s32[]{:S(2)}) async-start(), calls=%async_computation.11 | async-start | bytes 5308416 | tf_op jit(solution)/shard_map/all_gather | solution.py:70
  33.1 255.2 %all-gather.15.cloned.1.call-start = ((), (), s32[]{:S(2)}) async-start(), calls=%async_computation.12 | async-start | bytes 5308416 | tf_op jit(solution)/shard_map/all_gather | solution.py:72
  41.3 366.7 %reduce-scatter.20.cloned.1.call-start = ((), (), s32[]{:S(2)}) async-start(), calls=%async_computation.14 | async-start | bytes 1327104 | tf_op jit(solution)/shard_map/reduce_scatter | solution.py:191
  138.6 9.2 %copy-start.4 = (bf16[3,256,1,12,64]{1,4,3,0,2:T(8,128)(2,1)}, bf16[3,256,1,12,64]{1,4,3,0,2:T(8,128)(2,1)S(1)}, u32[]{:S(2)}) copy-start(bf16[3,256,1,12,64]{1,4,3,0,2:T(8,128)(2,1)S(1)} %copy.119) | copy-start | bytes 3538948
  142.7 7.4 copy-start.2
  150.2 3.6 copy-start
  150.2 3.7 copy-start.18
  150.2 3.7 copy-start.8
  153.9 2.9 copy-start.20
  156.8 2.3 copy-start.31
  159.1 4.6 copy-start.19
  159.1 4.6 copy-start.21
  162.4 125.9 %copy-start.6 = (f32[768,768]{1,0:T(8,128)}, f32[768,768]{1,0:T(8,128)S(1)}, u32[]{:S(2)}) copy-start(f32[768,768]{1,0:T(8,128)S(1)} %get-tuple-element.91) | copy-start | bytes 7077892
  288.4 8.1 copy-start.26
  296.0 3.6 slice-start.5
  296.5 3.1 slice-start.6
  298.2 15.1 %slice-start.3 = ((s8[4718592]{0:T(1024)(128)(4,1)}), s8[4194304]{0:T(1024)(128)(4,1)S(1)}, s32[]{:S(2)}) async-start(s8[4718592]{0:T(1024)(128)(4,1)} %bitcast.140), calls=%async_computation.25 | async-start | bytes 8388608
  299.6 13.7 %copy-start.12 = (f32[768,768]{1,0:T(8,128)}, f32[768,768]{1,0:T(8,128)S(1)}, u32[]{:S(2)}) copy-start(f32[768,768]{1,0:T(8,128)S(1)} %get-tuple-element.71) | copy-start | bytes 7077892
  299.6 13.7 %copy-start.7 = (f32[768,768]{1,0:T(8,128)S(1)}, f32[768,768]{1,0:T(8,128)}, u32[]{:S(2)}) copy-start(f32[768,768]{1,0:T(8,128)} %copy-done.6) | copy-start | bytes 7077892
  299.6 13.7 %copy-start.25 = (f32[768]{0:T(1024)S(1)}, f32[768]{0:T(1024)}, u32[]{:S(2)}) copy-start(f32[768]{0:T(1024)} %add_rsqrt_fusion.1) | copy-start | bytes 9220
  299.6 13.7 %slice-start.4 = ((s8[4718592]{0:T(1024)(128)(4,1)}), s8[524288]{0:T(1024)(128)(4,1)S(1)}, s32[]{:S(2)}) async-start(s8[4718592]{0:T(1024)(128)(4,1)} %bitcast.140), calls=%async_computation.26 | async-start | bytes 1048576
  321.0 2.9 copy-start.16
  339.4 144.0 %reduce-scatter.28.cloned.1.call-start = ((), (), s32[]{:S(2)}) async-start(), calls=%async_computation.18 | async-start | bytes 3981312
  339.5 7.9 copy-start.17
  347.4 6.9 copy-start.3
  347.4 9.4 %slice-start = ((s8[9437184]{0:T(1024)(128)(4,1)}), s8[4194304]{0:T(1024)(128)(4,1)S(1)}, s32[]{:S(2)}) async-start(s8[9437184]{0:T(1024)(128)(4,1)} %bitcast.114), calls=%async_computation.22 | async-start | bytes 8388608
  347.4 9.4 %slice-start.1 = ((s8[9437184]{0:T(1024)(128)(4,1)}), s8[4194304]{0:T(1024)(128)(4,1)S(1)}, s32[]{:S(2)}) async-start(s8[9437184]{0:T(1024)(128)(4,1)} %bitcast.114), calls=%async_computation.23 | async-start | bytes 8388608
  354.3 2.5 slice-start.2
  364.4 2.9 copy-start.14
  377.4 204.5 %reduce-scatter.26.cloned.1.call-start = ((), (), s32[]{:S(2)}) async-start(), calls=%async_computation.17 | async-start | bytes 5308416 | tf_op jit(solution)/shard_map/reduce_scatter | solution.py:200
  386.9 294.1 %reduce-scatter.22.cloned.1.call-start = ((), (), s32[]{:S(2)}) async-start(), calls=%async_computation.15 | async-start | bytes 5308416 | tf_op jit(solution)/shard_map/reduce_scatter | solution.py:194
  397.1 348.6 %reduce-scatter.34.cloned.1.call-start = ((), (), s32[]{:S(2)}) async-start(), calls=%async_computation.21 | async-start | bytes 221184
  397.4 192.6 %copy-start.15 = (bf16[3,256,768]{2,1,0:T(8,128)(2,1)S(1)}, bf16[3,256,768]{2,1,0:T(8,128)(2,1)}, u32[]{:S(2)}) copy-start(bf16[3,256,768]{2,1,0:T(8,128)(2,1)} %param.11) | copy-start | bytes 3538948
  407.9 359.5 %reduce-scatter.30.cloned.1.call-start = ((), (), s32[]{:S(2)}) async-start(), calls=%async_computation.19 | async-start | bytes 245760
  409.8 382.2 %reduce-scatter.18.cloned.1.call-start = ((), (), s32[]{:S(2)}) async-start(), calls=%async_computation.13 | async-start | bytes 737280 | tf_op jit(solution)/shard_map/reduce_scatter | solution.py:208
  485.5 330.9 %reduce-scatter.32.cloned.1.call-start = ((), (), s32[]{:S(2)}) async-start(), calls=%async_computation.20 | async-start | bytes 737280
  584.1 256.9 %reduce-scatter.24.cloned.1.call-start = ((), (), s32[]{:S(2)}) async-start(), calls=%async_computation.16 | async-start | bytes 737280 | tf_op jit(solution)/shard_map/reduce_scatter | solution.py:214
  590.0 93.6 %copy-start.29 = (bf16[3072]{0:T(1024)(128)(2,1)S(1)}, bf16[3072]{0:T(1024)(128)(2,1)}, u32[]{:S(2)}) copy-start(bf16[3072]{0:T(1024)(128)(2,1)} %get-tuple-element.98) | copy-start | bytes 18436
  (8 other events, 10.8 us)
Sparse Core Ops, SparseCore 0:
  17.7 66.3 all-gather.8
  86.8 39.5 all-gather.10
  128.6 78.6 all-gather.12
  209.2 79.1 all-gather.14
  339.6 62.2 reduce-scatter.19
  405.3 78.0 reduce-scatter.27
  487.1 94.8 reduce-scatter.25
  585.6 95.3 reduce-scatter.21
  684.9 60.8 reduce-scatter.33
  748.6 18.7 reduce-scatter.29
  769.9 22.0 reduce-scatter.17
  794.3 22.0 reduce-scatter.31
  819.0 22.0 reduce-scatter.23
where the time goes:
time: 854 us; the launch traced here: 849 us
  waiting for transfers between devices  472 us (55%)
  matrix products  122 us (14%)
  blocking collectives  121 us (14%)
  local copies, waits for them, and re-layouts  87.1 us (10%)
  other arithmetic  29 us (3%)
  between operations  17.4 us (2%)
    unnamed x17, waiting for transfers between devices  144 us
    reduce_scatter x1, waiting for transfers between devices, local(): lax.psum_scatter(grad_down.astype(jnp.bfloat16), 'dp', scatter_dimension=...  96.3 us
    reduce_scatter x1, waiting for transfers between devices, local(): lax.psum_scatter(grad_up.astype(jnp.bfloat16), 'dp', scatter_dimension=0,...  89.9 us
    all_gather x1, waiting for transfers between devices, local(): lax.all_gather(down_part, 'dp', axis=0, tiled=True)  52.6 us
    unnamed x109, local copies, waits for them, and re-layouts  42.9 us
    all_gather x1, waiting for transfers between devices, local(): lax.all_gather(up_part, 'dp', axis=0, tiled=True)  42.9 us
    unnamed x3, blocking collectives  32.4 us
    dot_general x1, matrix products, local(): jnp.dot(first_norm, w_up, preferred_element_type=jnp.float32)  28.5 us
  transfers between devices with their start and end apart: 13, of which 10 were waited for; matrix products, arithmetic and copies ran while one was open for 21% of the time, Pallas kernels for 0%

commit v1 on v0

v1 whole, which is shorter than its diff:
```python
import itertools
from functools import partial

import jax
import jax.numpy as jnp
from jax import lax
from jax.experimental import pallas as pl
from jax.experimental.pallas import tpu as pltpu
from jax.sharding import PartitionSpec as P

HEAD_DIM = 64
EPS = 1e-05
MASKED = -1000000000.0
F32 = jnp.float32
BF16 = jnp.bfloat16
VMEM_LIMIT = 56 * 1024 * 1024
LANES = 128


class Links:
    def __init__(self, n_dp, n_fsdp):
        self.n_dp, self.n_fsdp = n_dp, n_fsdp
        self.high = n_fsdp // 4
        self.rest = (n_dp // 2) * self.high

    def number(self, rest, y, x, core):
        z, high = divmod(rest, self.high)
        return (z * 2 + y) * self.n_fsdp + (high * 2 + x) * 2 + core

    def pairs(self, step):
        return [
            (self.number(*place), self.number(*step(*place)))
            for place in itertools.product(range(self.rest), range(2), range(2), range(2))
        ]

    def move(self, value, step):
        return lax.ppermute(value, ("dp", "fsdp"), self.pairs(step))

    def core(self, value):
        return self.move(value, lambda q, y, x, c: (q, y, x, 1 - c))

    def along_x(self, value):
        return self.move(value, lambda q, y, x, c: (q, y, 1 - x, c))

    def along_y(self, value):
        return self.move(value, lambda q, y, x, c: (q, 1 - y, x, c))

    def first(self, value):
        return self.move(value, lambda q, y, x, c: (q, 1 - y, x, c) if c else (q, y, 1 - x, c))

    def second(self, value):
        return self.move(value, lambda q, y, x, c: (q, y, 1 - x, c) if c else (q, 1 - y, x, c))

    def ahead(self, value, far):
        return self.move(value, lambda q, y, x, c: ((q + far) % self.rest, y, x, c))

    def place(self):
        dp, fsdp = lax.axis_index("dp"), lax.axis_index("fsdp")
        rest = (dp // 2) * self.high + fsdp // 4
        return rest, dp % 2, (fsdp // 2) % 2, fsdp % 2


def chip_piece(links, shard, core):
    half = shard.shape[0] // 2
    keep = lax.dynamic_slice_in_dim(shard, core * half, half, 0)
    give = lax.dynamic_slice_in_dim(shard, (1 - core) * half, half, 0)
    got = links.core(give)
    return jnp.where(
        core == 0, jnp.concatenate([keep, got], axis=1), jnp.concatenate([got, keep], axis=1)
    )


def spread(links, piece):
    own = jnp.stack([piece] + [links.ahead(piece, far) for far in range(1, links.rest)])
    by_first = links.first(own)
    by_second = links.second(own)
    by_both = links.second(by_first)
    near = [own, by_second, by_first, by_both]
    return near + [links.core(item) for item in near]


def collect(links, keep, give):
    got = links.core(give)
    far_half = (keep[1].astype(F32) + got[1].astype(F32)).astype(BF16)
    by_second = links.second(far_half)

    def near(one):
        return keep[0, one].astype(F32) + got[0, one].astype(F32) + by_second[one].astype(F32)

    by_first = links.first(near(1).astype(BF16))
    blocks = [near(0)[far] + by_first[far].astype(F32) for far in range(links.rest)]
    total = blocks[0]
    for far in range(1, links.rest):
        total = total + links.ahead(blocks[far].astype(BF16), far).astype(F32)
    return total


def owned(links, piece, core):
    width = piece.shape[1] // 2
    keep = lax.dynamic_slice_in_dim(piece, core * width, width, 1)
    give = lax.dynamic_slice_in_dim(piece, (1 - core) * width, width, 1)
    got = links.core(give)
    return jnp.where(
        core == 0, jnp.concatenate([keep, got], axis=0), jnp.concatenate([got, keep], axis=0)
    )


def sum_everywhere(links, value):
    value = value + links.core(value)
    value = value + links.along_x(value)
    value = value + links.along_y(value)
    total = value
    for far in range(1, links.rest):
        total = total + links.ahead(value, far)
    return total


class Blocks:
    def __init__(self, links, where):
        self.links = links
        self.rest, self.y, self.x, self.core = where[0], where[1], where[2], where[3]

    def device(self, other, one, two, far, sign):
        links = self.links
        core = jnp.bitwise_xor(self.core, other)
        flip_x = jnp.where(core == 0, one, two)
        flip_y = jnp.where(core == 0, two, one)
        rest = lax.rem(self.rest + (sign * far + links.rest), links.rest)
        x, y = jnp.bitwise_xor(self.x, flip_x), jnp.bitwise_xor(self.y, flip_y)
        dp = lax.div(rest, links.high) * 2 + y
        return dp, lax.rem(rest, links.high) * 2 + x, core

    def corner(self, rows, cols, *spot):
        dp, wide, core = self.device(*spot)
        return pl.multiple_of((dp * 2 + core) * rows, rows), pl.multiple_of(wide * cols, cols)


def load_weight(links, where, refs, first_col, cols, out, sem):
    if len(refs) == 1:
        copies = [pltpu.make_async_copy(refs[0], out, sem)]
    else:
        blocks = Blocks(links, where)
        rows = refs[0].shape[1]
        copies = []
        for stack, far in itertools.product(range(8), range(links.rest)):
            row, col = blocks.corner(
                rows, cols, stack // 4, (stack // 2) % 2, stack % 2, far, -1
            )
            copies.append(
                pltpu.make_async_copy(
                    refs[stack].at[far, :, pl.ds(first_col, cols)],
                    out.at[pl.ds(row, rows), pl.ds(col, cols)],
                    sem,
                )
            )
    for copy in copies:
        copy.start()
    return copies


def store_grad(links, where, grad, refs, first_col, cols, sem):
    if len(refs) == 1:
        copies = [pltpu.make_async_copy(grad, refs[0], sem)]
    else:
        blocks = Blocks(links, where)
        rows = refs[0].shape[3]
        copies = []
        for other, one, two, far in itertools.product(
            range(2), range(2), range(2), range(links.rest)
        ):
            row, col = blocks.corner(rows, cols, other, one, two, far, 1)
            copies.append(
                pltpu.make_async_copy(
                    grad.at[pl.ds(row, rows), pl.ds(col, cols)],
                    refs[other].at[two, one, far, :, pl.ds(first_col, cols)],
                    sem,
                )
            )
    for copy in copies:
        copy.start()
    return copies


def wait_all(copies):
    for copy in copies:
        copy.wait()


def dot(left, right):
    return lax.dot_general(left, right, (((1,), (0,)), ((), ())), preferred_element_type=F32)


def dot_nt(left, right):
    return lax.dot_general(left, right, (((1,), (1,)), ((), ())), preferred_element_type=F32)


def dot_tn(left, right):
    return lax.dot_general(left, right, (((0,), (0,)), ((), ())), preferred_element_type=F32)


def normalize(hidden):
    centered = hidden - jnp.mean(hidden, axis=-1, keepdims=True)
    factor = lax.rsqrt(jnp.mean(centered * centered, axis=-1, keepdims=True) + EPS)
    return centered * factor, factor


def norm_back(scaled, normed, factor):
    return factor * (
        scaled
        - jnp.mean(scaled, axis=-1, keepdims=True)
        - normed * jnp.mean(scaled * normed, axis=-1, keepdims=True)
    )


def gelu_parts(value):
    size = jnp.abs(value) * 0.7071067811865476
    bell = jnp.exp(-0.5 * value * value)
    part = 1.0 / (1.0 + 0.3275911 * size)
    poly = part * (
        0.127414796
        + part * (-0.142248368 + part * (0.7107068705 + part * (-0.7265760135 + part * 0.5307027145)))
    )
    tail = poly * bell
    weight = jnp.where(value > 0.0, 1.0 - tail, tail)
    return value * weight, weight + value * (bell * 0.3989422804014327)


def small_kernel(links, where, *refs):
    stacks, vec_out, bias_out, held, sem = refs[:8], *refs[8:]
    blocks = Blocks(links, where)
    first_col = stacks[0].shape[2] - LANES
    copies = []
    for stack, far in itertools.product(range(8), range(links.rest)):
        dp, wide, core = blocks.device(stack // 4, (stack // 2) % 2, stack % 2, far, -1)
        copies.append(
            pltpu.make_async_copy(
                stacks[stack].at[far, pl.ds(0, 16), pl.ds(first_col, LANES)],
                held.at[dp * links.n_fsdp + wide * 2 + core],
                sem,
            )
        )
    for copy in copies:
        copy.start()
    wait_all(copies)
    rows, width = 8 // links.n_fsdp, vec_out.shape[1] // links.n_dp
    got = [held[at].astype(F32)[:, :width] for at in range(links.n_dp * links.n_fsdp)]
    for fsdp in range(links.n_fsdp):
        line = jnp.concatenate([got[dp * links.n_fsdp + fsdp] for dp in range(links.n_dp)], axis=1)
        vec_out[pl.ds(rows * fsdp, rows), :] = line[:rows]
    bias_out[...] = jnp.concatenate(got, axis=1)[rows : rows + 1]


def head_half(pair, half):
    lane = lax.broadcasted_iota(jnp.int32, pair.shape, 1)
    keep = (lane < HEAD_DIM) if half == 0 else (lane >= HEAD_DIM)
    return jnp.where(keep, pair, jnp.zeros_like(pair))


def join_halves(low, high):
    lane = lax.broadcasted_iota(jnp.int32, low.shape, 1)
    return jnp.where(lane < HEAD_DIM, low, high)


def attend_kernel(links, n_weight, where, lengths, tokens, vec, *refs):
    weight_refs = refs[:n_weight]
    out_refs = refs[n_weight : 2 * n_weight]
    qkv, attended, first_norm, normed, factor = refs[2 * n_weight : 2 * n_weight + 5]
    w_qkv, w_out, sems = refs[2 * n_weight + 5 :]
    width = tokens.shape[1]
    seq = 256
    sents = tokens.shape[0] // seq
    wide = width * 3 * 2 // links.n_fsdp
    copies = load_weight(links, where, weight_refs, 0, wide, w_qkv, sems.at[0])
    copies_out = load_weight(
        links, where, out_refs, wide, width * 2 // links.n_fsdp, w_out, sems.at[1]
    )
    wait_all(copies)

    def project(tile, carry):
        at = pl.ds(pl.multiple_of(tile * 256, 256), 256)
        product = dot(tokens[...], w_qkv[:, at])
        place = tile * 256
        row = jnp.where(place < width, 0, 1)
        col = pl.multiple_of(lax.rem(place, width), 256)
        bias = vec[pl.ds(row, 1), pl.ds(col, 256)]
        bias = jnp.where((place >= width) & (place < 2 * width), 0.0, bias)
        qkv[:, at] = (product + bias).astype(BF16)
        return carry

    lax.fori_loop(0, 3 * width // 256, project, 0)

    pairs = width // LANES

    def attend(step, carry):
        sent, pair = lax.div(step, pairs), lax.rem(step, pairs)
        rows = pl.ds(pl.multiple_of(sent * seq, seq), seq)
        col = pl.multiple_of(pair * LANES, LANES)
        queries = qkv[rows, pl.ds(col, LANES)]
        keys = qkv[rows, pl.ds(col + width, LANES)]
        values = qkv[rows, pl.ds(col + 2 * width, LANES)]
        queries = queries * jnp.asarray(HEAD_DIM ** (-0.5), BF16)
        keep = lax.broadcasted_iota(jnp.int32, (seq, seq), 1) < lengths[sent]
        outs = []
        for half in range(2):
            scores = jnp.where(keep, dot_nt(head_half(queries, half), keys), MASKED)
            exponent = jnp.exp(scores - jnp.max(scores, axis=-1, keepdims=True))
            scale = 1.0 / jnp.sum(exponent, axis=-1, keepdims=True)
            outs.append(dot((exponent * scale).astype(BF16), values))
        attended[rows, pl.ds(col, LANES)] = join_halves(*outs).astype(BF16)
        return carry

    lax.fori_loop(0, sents * pairs, attend, 0)
    wait_all(copies_out)
    for sent in range(sents):
        rows = pl.ds(sent * seq, seq)
        hidden = tokens[rows, :].astype(F32) + (dot(attended[rows, :], w_out[...]) + vec[2:3, :])
        part, scale = normalize(hidden)
        normed[rows, :] = part
        factor[rows, :] = jnp.broadcast_to(scale, (seq, LANES))
        first_norm[rows, :] = (part * vec[3:4, :] + vec[4:5, :]).astype(BF16)


def up_kernel(links, n_weight, where, first_norm, bias, *refs):
    weight_refs = refs[:n_weight]
    activated, slope = refs[n_weight : n_weight + 2]
    w_up, act_buf, slope_buf, sems, out_sems = refs[n_weight + 2 :]
    width, hidden = w_up.shape
    copies = load_weight(links, where, weight_refs, 0, hidden * 2 // links.n_fsdp, w_up, sems.at[0])
    wait_all(copies)
    tile = 256
    count = hidden // tile

    def out_copies(step):
        at = pl.ds(pl.multiple_of(step * tile, tile), tile)
        slot = lax.rem(step, 2)
        return (
            pltpu.make_async_copy(act_buf.at[slot], activated.at[:, at], out_sems.at[slot, 0]),
            pltpu.make_async_copy(slope_buf.at[slot], slope.at[:, at], out_sems.at[slot, 1]),
        )

    def body(step, carry):
        at = pl.ds(pl.multiple_of(step * tile, tile), tile)
        slot = lax.rem(step, 2)

        @pl.when(step >= 2)
        def _():
            wait_all(out_copies(step - 2))

        for part in range(first_norm.shape[0] // 256):
            rows = pl.ds(part * 256, 256)
            value = dot(first_norm[rows, :], w_up[:, at]) + bias[:, at]
            act, der = gelu_parts(value)
            act_buf[slot, rows, :] = act.astype(BF16)
            slope_buf[slot, rows, :] = der.astype(BF16)
        for copy in out_copies(step):
            copy.start()
        return carry

    lax.fori_loop(0, count, body, 0)
    wait_all(out_copies(count - 2))
    wait_all(out_copies(count - 1))


def down_kernel(links, n_weight, n_grad, where, lengths, depth, prefix, *refs):
    activated, first_norm, tokens, cotangent, vec = refs[:5]
    weight_refs = refs[5 : 5 + n_weight]
    layer_out, pooled, d_second, d_down, sums = refs[5 + n_weight : 10 + n_weight]
    grad_refs = refs[10 + n_weight : 10 + n_weight + n_grad]
    w_down, grad, sems = refs[10 + n_weight + n_grad :]
    hidden, width = w_down.shape
    seq = 256
    sents = tokens.shape[0] // seq
    cols = width * 2 // links.n_fsdp
    wait_all(load_weight(links, where, weight_refs, 0, cols, w_down, sems.at[0]))
    sums[...] = jnp.zeros_like(sums)
    columns = lax.broadcasted_iota(jnp.int32, (1, width), 1)
    for sent in range(sents):
        rows = pl.ds(sent * seq, seq)
        total = first_norm[rows, :].astype(F32) + (dot(activated[rows, :], w_down[...]) + vec[5:6, :])
        normed, factor = normalize(total)
        result = normed * vec[6:7, :] + vec[7:8, :]
        layer_out[rows, :] = result.astype(BF16)
        valid = lax.broadcasted_iota(jnp.int32, (seq, width), 0) < lengths[sent]
        source = jnp.where(depth[sent] == 1, result, tokens[rows, :].astype(F32))
        mean = jnp.sum(jnp.where(valid, source, 0.0), axis=0, keepdims=True)
        mean = mean / lengths[sent].astype(F32)
        for at in range(pooled.shape[1]):
            pooled[sent, pl.ds(at, 1), :] = mean * (columns < prefix[at]).astype(F32)
        grad_in = cotangent[rows, :].astype(F32)
        sums[0:1, :] += jnp.sum(grad_in * normed, axis=0, keepdims=True)
        sums[1:2, :] += jnp.sum(grad_in, axis=0, keepdims=True)
        back = norm_back(grad_in * vec[6:7, :], normed, factor)
        d_second[rows, :] = back
        low = back.astype(BF16)
        d_down[rows, :] = low
        sums[2:3, :] += jnp.sum(low.astype(F32), axis=0, keepdims=True)

    def body(step, carry):
        at = pl.ds(pl.multiple_of(step * 256, 256), 256)
        grad[at, :] = dot_tn(activated[:, at], d_down[...]).astype(BF16)
        return carry

    lax.fori_loop(0, hidden // 256, body, 0)
    wait_all(store_grad(links, where, grad, grad_refs, 0, cols, sems.at[1]))


def up_back_kernel(links, n_weight, n_grad, where, d_down, slope, first_norm, *refs):
    weight_refs = refs[:n_weight]
    d_pre, sums = refs[n_weight : n_weight + 2]
    grad_refs = refs[n_weight + 2 : n_weight + 2 + n_grad]
    w_down, turned, grad, sems = refs[n_weight + 2 + n_grad :]
    hidden, width = w_down.shape
    copies = load_weight(links, where, weight_refs, 0, width * 2 // links.n_fsdp, w_down, sems.at[0])
    turned[...] = first_norm[...].T
    wait_all(copies)

    def body(step, carry):
        at = pl.ds(pl.multiple_of(step * 256, 256), 256)
        d_act = dot_nt(d_down[...], w_down[at, :])
        low = (d_act * slope[:, at].astype(F32)).astype(BF16)
        d_pre[:, at] = low
        sums[:, at] = jnp.sum(low.astype(F32), axis=0, keepdims=True)
        grad[:, at] = dot(turned[...], low).astype(BF16)
        return carry

    lax.fori_loop(0, hidden // 256, body, 0)
    wait_all(store_grad(links, where, grad, grad_refs, 0, hidden * 2 // links.n_fsdp, sems.at[1]))


def out_back_kernel(links, n_weight, where, *refs):
    d_pre, d_second, normed, factor, attended, vec = refs[:6]
    up_refs = refs[6 : 6 + n_weight]
    out_refs = refs[6 + n_weight : 6 + 2 * n_weight]
    d_resid, d_att, grad_out, sums = refs[6 + 2 * n_weight : 10 + 2 * n_weight]
    w_up, w_out, d_attn, sems = refs[10 + 2 * n_weight :]
    width, hidden = w_up.shape
    seq = 256
    wide = width * 3 * 2 // links.n_fsdp
    copies = load_weight(links, where, up_refs, 0, hidden * 2 // links.n_fsdp, w_up, sems.at[0])
    copies_out = load_weight(
        links, where, out_refs, wide, width * 2 // links.n_fsdp, w_out, sems.at[1]
    )
    wait_all(copies)
    sums[...] = jnp.zeros_like(sums)
    for part in range(d_pre.shape[0] // seq):
        rows = pl.ds(part * seq, seq)
        d_first = dot_nt(d_pre[rows, :], w_up[...]) + d_second[rows, :]
        unit = normed[rows, :]
        sums[0:1, :] += jnp.sum(d_first * unit, axis=0, keepdims=True)
        sums[1:2, :] += jnp.sum(d_first, axis=0, keepdims=True)
        back = norm_back(d_first * vec[3:4, :], unit, factor[rows, 0:1])
        d_resid[rows, :] = back
        low = back.astype(BF16)
        d_attn[rows, :] = low
        sums[2:3, :] += jnp.sum(low.astype(F32), axis=0, keepdims=True)
    wait_all(copies_out)
    d_att[...] = dot_nt(d_attn[...], w_out[...]).astype(BF16)
    grad_out[...] = dot_tn(attended[...], d_attn[...]).astype(BF16)


def attend_back_kernel(links, n_grad, where, lengths, qkv, d_att, tokens, grad_out, *refs):
    d_qkv, sums = refs[:2]
    grad_refs = refs[2 : 2 + n_grad]
    turned, grad, sems = refs[2 + n_grad :]
    width = tokens.shape[1]
    seq = 256
    sents = tokens.shape[0] // seq
    pairs = width // LANES
    wide = width * 3 * 2 // links.n_fsdp
    if n_grad == 2:
        copies = store_grad(
            links, where, grad_out, grad_refs, wide, width * 2 // links.n_fsdp, sems.at[0]
        )
    else:
        copies = []
    turned[...] = tokens[...].T
    sums[...] = jnp.zeros_like(sums)
    key_scale = jnp.asarray(HEAD_DIM ** (-0.5), BF16)

    def body(step, carry):
        sent, pair = lax.div(step, pairs), lax.rem(step, pairs)
        rows = pl.ds(pl.multiple_of(sent * seq, seq), seq)
        col = pl.multiple_of(pair * LANES, LANES)
        queries = qkv[rows, pl.ds(col, LANES)] * key_scale
        keys = qkv[rows, pl.ds(col + width, LANES)]
        values = qkv[rows, pl.ds(col + 2 * width, LANES)]
        d_out = d_att[rows, pl.ds(col, LANES)]
        keep = lax.broadcasted_iota(jnp.int32, (seq, seq), 0) < lengths[sent]
        d_queries, d_keys, d_values = [], [], []
        for half in range(2):
            scores = jnp.where(keep, dot_nt(keys, head_half(queries, half)), MASKED)
            exponent = jnp.exp(scores - jnp.max(scores, axis=0, keepdims=True))
            probs = exponent * (1.0 / jnp.sum(exponent, axis=0, keepdims=True))
            d_values.append(dot(probs.astype(BF16), d_out))
            d_probs = dot_nt(values, head_half(d_out, half))
            row_dot = jnp.sum(d_probs * probs, axis=0, keepdims=True)
            d_scores = (probs * (d_probs - row_dot)).astype(BF16)
            d_keys.append(dot(d_scores, queries))
            d_queries.append(dot_tn(d_scores, keys))
        d_query = (join_halves(*d_queries) * (HEAD_DIM ** (-0.5))).astype(BF16)
        d_value = join_halves(*d_values).astype(BF16)
        d_qkv[rows, pl.ds(col, LANES)] = d_query
        d_qkv[rows, pl.ds(col + width, LANES)] = join_halves(*d_keys).astype(BF16)
        d_qkv[rows, pl.ds(col + 2 * width, LANES)] = d_value
        sums[0:1, pl.ds(col, LANES)] += jnp.sum(d_query.astype(F32), axis=0, keepdims=True)
        sums[1:2, pl.ds(col, LANES)] += jnp.sum(d_value.astype(F32), axis=0, keepdims=True)
        return carry

    lax.fori_loop(0, sents * pairs, body, 0)

    def grads(step, carry):
        at = pl.ds(pl.multiple_of(step * 256, 256), 256)
        grad[:, at] = dot(turned[...], d_qkv[:, at]).astype(BF16)
        return carry

    lax.fori_loop(0, 3 * width // 256, grads, 0)
    wait_all(copies)
    wait_all(store_grad(links, where, grad, grad_refs, 0, wide, sems.at[1]))


def inputs_kernel(links, n_weight, where, d_qkv, d_resid, *refs):
    weight_refs = refs[:n_weight]
    grad_tokens, w_qkv, sem = refs[n_weight:]
    width = d_resid.shape[1]
    wait_all(load_weight(links, where, weight_refs, 0, width * 3 * 2 // links.n_fsdp, w_qkv, sem))
    for part in range(d_qkv.shape[0] // 256):
        rows = pl.ds(part * 256, 256)
        grad_tokens[rows, :] = (dot_nt(d_qkv[rows, :], w_qkv[...]) + d_resid[rows, :]).astype(BF16)


SMEM_SPEC = pl.BlockSpec(memory_space=pltpu.SMEM)
VMEM_SPEC = pl.BlockSpec(memory_space=pltpu.VMEM)
ANY_SPEC = pl.BlockSpec(memory_space=pl.ANY)


def call(body, name, outs, scratch, args, flops):
    spec = {"s": SMEM_SPEC, "v": VMEM_SPEC, "a": ANY_SPEC}
    size = sum(v.size * v.dtype.itemsize for _, v in list(args) + list(outs))
    return pl.pallas_call(
        body,
        name=name,
        out_shape=[jax.ShapeDtypeStruct(v.shape, v.dtype) for _, v in outs],
        in_specs=[spec[place] for place, _ in args],
        out_specs=[spec[place] for place, _ in outs],
        scratch_shapes=scratch,
        compiler_params=pltpu.CompilerParams(vmem_limit_bytes=VMEM_LIMIT),
        cost_estimate=pl.CostEstimate(flops=flops, bytes_accessed=size, transcendentals=0),
    )(*[value for _, value in args])


def shaped(*shape, dtype=BF16):
    return jax.ShapeDtypeStruct(shape, dtype)


def local(
    n_dp,
    n_fsdp,
    tokens,
    qkv_weight,
    out_weight,
    up_weight,
    up_bias,
    down_weight,
    vectors,
    lengths,
    exit_depth,
    prefix_widths,
    cotangent,
):
    sent_count, seq_len, width = tokens.shape
    rows = sent_count * seq_len
    hidden = up_weight.shape[1] * n_fsdp
    links = Links(n_dp, n_fsdp)
    where = jnp.stack(links.place()).astype(jnp.int32)
    core = where[3]
    inputs = tokens.reshape(rows, width)
    grad_in = cotangent.reshape(rows, width)
    blocked = qkv_weight.shape[0] % 32 == 0 and out_weight.shape[1] % 64 == 0

    if blocked:
        small = jnp.concatenate([vectors, up_bias.reshape(1, -1)], axis=0)
        half = qkv_weight.shape[0] // 2
        small = jnp.pad(small, ((0, half - small.shape[0]), (0, LANES - small.shape[1])))
        piece = jnp.concatenate(
            [chip_piece(links, qkv_weight, core), chip_piece(links, out_weight, core), small], axis=1
        )
        stacks_in = spread(links, piece)
        stacks_up = spread(links, chip_piece(links, up_weight, core))
        stacks_down = spread(links, chip_piece(links, down_weight, core))
        any_in = [("a", item) for item in stacks_in]
        any_out = any_in
        any_up = [("a", item) for item in stacks_up]
        any_down = [("a", item) for item in stacks_down]
        vec, bias = call(
            partial(small_kernel, links),
            "small_values",
            [("v", shaped(8, width, dtype=F32)), ("v", shaped(1, hidden, dtype=F32))],
            [pltpu.VMEM((n_dp * n_fsdp, 16, LANES), BF16), pltpu.SemaphoreType.DMA],
            [("s", where)] + any_in,
            1000,
        )
    else:

        def whole(shard):
            part = lax.all_gather(shard, "fsdp", axis=1, tiled=True)
            return lax.all_gather(part, "dp", axis=0, tiled=True)

        any_in, any_out, any_up, any_down = (
            [("a", whole(shard))] for shard in (qkv_weight, out_weight, up_weight, down_weight)
        )
        vec = lax.all_gather(vectors, "fsdp", axis=0, tiled=True)
        vec = lax.all_gather(vec, "dp", axis=1, tiled=True).astype(F32)
        bias = lax.all_gather(up_bias, ("dp", "fsdp"), axis=0, tiled=True)
        bias = bias.astype(F32).reshape(1, hidden)
    n_weight = len(any_in)
    n_grad = 2 if blocked else 1

    def grad_outs(shard, extra=0):
        if not blocked:
            return [("a", shaped(shard.shape[0] * n_dp, shard.shape[1] * n_fsdp))]
        shape = (2, 2, links.rest, shard.shape[0] // 2, shard.shape[1] * 2 + extra)
        return [("a", shaped(*shape))] * 2

    one, two = pltpu.SemaphoreType.DMA, pltpu.SemaphoreType.DMA((2,))
    flat = shaped(rows, width)
    flat32 = shaped(rows, width, dtype=F32)
    lined = ("s", where)

    qkv, attended, first_norm, normed, factor = call(
        partial(attend_kernel, links, n_weight),
        "attend",
        [
            ("v", shaped(rows, 3 * width)),
            ("v", flat),
            ("v", flat),
            ("v", flat32),
            ("v", shaped(rows, LANES, dtype=F32)),
        ],
        [pltpu.VMEM((width, 3 * width), BF16), pltpu.VMEM((width, width), BF16), two],
        [lined, ("s", lengths), ("v", inputs), ("v", vec)] + any_in + any_out,
        8 * rows * width * width + 4 * rows * seq_len * width,
    )
    activated, slope = call(
        partial(up_kernel, links, n_weight),
        "up",
        [("a", shaped(rows, hidden)), ("a", shaped(rows, hidden))],
        [
            pltpu.VMEM((width, hidden), BF16),
            pltpu.VMEM((2, rows, 256), BF16),
            pltpu.VMEM((2, rows, 256), BF16),
            two,
            pltpu.SemaphoreType.DMA((2, 2)),
        ],
        [lined, ("v", first_norm), ("v", bias)] + any_up,
        2 * rows * width * hidden,
    )
    down = call(
        partial(down_kernel, links, n_weight, n_grad),
        "down",
        [
            ("v", flat),
            ("v", shaped(sent_count, prefix_widths.shape[0], width, dtype=F32)),
            ("v", flat32),
            ("v", flat),
            ("v", shaped(8, width, dtype=F32)),
        ]
        + grad_outs(down_weight),
        [pltpu.VMEM((hidden, width), BF16), pltpu.VMEM((hidden, width), BF16), two],
        [lined, ("s", lengths), ("s", exit_depth), ("s", prefix_widths)]
        + [("v", activated), ("v", first_norm), ("v", inputs), ("v", grad_in), ("v", vec)]
        + any_down,
        4 * rows * width * hidden,
    )
    layer_out, pooled, d_second, d_down, sums_down = down[:5]
    grad_down = down[5:]

    up_back = call(
        partial(up_back_kernel, links, n_weight, n_grad),
        "up_back",
        [("v", shaped(rows, hidden)), ("v", shaped(1, hidden, dtype=F32))] + grad_outs(up_weight),
        [
            pltpu.VMEM((hidden, width), BF16),
            pltpu.VMEM((width, rows), BF16),
            pltpu.VMEM((width, hidden), BF16),
            two,
        ],
        [lined, ("v", d_down), ("v", slope), ("v", first_norm)] + any_down,
        4 * rows * width * hidden,
    )
    d_pre, sums_up = up_back[:2]
    grad_up = up_back[2:]
    d_resid, d_att, grad_out, sums_out = call(
        partial(out_back_kernel, links, n_weight),
        "out_back",
        [("v", flat32), ("v", flat), ("v", shaped(width, width)), ("v", shaped(8, width, dtype=F32))],
        [
            pltpu.VMEM((width, hidden), BF16),
            pltpu.VMEM((width, width), BF16),
            pltpu.VMEM((rows, width), BF16),
            two,
        ],
        [lined]
        + [("v", item) for item in (d_pre, d_second, normed, factor, attended, vec)]
        + any_up
        + any_out,
        2 * rows * width * hidden + 4 * rows * width * width,
    )
    attend_back = call(
        partial(attend_back_kernel, links, n_grad),
        "attend_back",
        [("v", shaped(rows, 3 * width)), ("v", shaped(8, width, dtype=F32))]
        + grad_outs(qkv_weight, 2 * out_weight.shape[1]),
        [pltpu.VMEM((width, rows), BF16), pltpu.VMEM((width, 3 * width), BF16), two],
        [lined, ("s", lengths), ("v", qkv), ("v", d_att), ("v", inputs), ("v", grad_out)],
        6 * rows * width * width + 10 * rows * seq_len * width,
    )
    d_qkv, sums_in = attend_back[:2]
    grad_in_blocks = attend_back[2:]
    (grad_tokens,) = call(
        partial(inputs_kernel, links, n_weight),
        "inputs",
        [("v", flat)],
        [pltpu.VMEM((width, 3 * width), BF16), one],
        [lined, ("v", d_qkv), ("v", d_resid)] + any_in,
        6 * rows * width * width,
    )

    grad_vec = jnp.concatenate(
        [sums_in[:2], sums_out[2:3], sums_out[:2], sums_down[2:3], sums_down[:2]], axis=0
    )
    if blocked:
        own_down = owned(links, collect(links, *grad_down), core)
        own_up = owned(links, collect(links, *grad_up), core)
        last = collect(links, *grad_in_blocks)
        split = 2 * qkv_weight.shape[1]
        own_qkv = owned(links, last[:, :split], core)
        own_out = owned(links, last[:, split:], core)
    else:

        def scattered(grad):
            part = lax.psum_scatter(grad, "dp", scatter_dimension=0, tiled=True)
            part = lax.psum_scatter(part, "fsdp", scatter_dimension=1, tiled=True)
            return part.astype(F32)

        own_down, own_up, own_out, own_qkv = (
            scattered(item) for item in (grad_down[0], grad_up[0], grad_out, grad_in_blocks[0])
        )
    every = jnp.concatenate([grad_vec, sums_up.reshape(-1, width)], axis=0)
    every = sum_everywhere(links, every)
    dp, fsdp = lax.axis_index("dp"), lax.axis_index("fsdp")
    own_vec = lax.dynamic_slice(
        every, (fsdp * vectors.shape[0], dp * vectors.shape[1]), vectors.shape
    )
    own_bias = lax.dynamic_slice_in_dim(
        every[8:].reshape(-1), (dp * n_fsdp + fsdp) * up_bias.shape[0], up_bias.shape[0], 0
    )
    return (
        layer_out.reshape(tokens.shape),
        pooled,
        grad_tokens.reshape(tokens.shape),
        own_qkv,
        own_out,
        own_up,
        own_bias,
        own_down,
        own_vec,
    )


def solution(mesh):
    placed = (
        P(("dp", "fsdp"), None, None),
        P("dp", "fsdp"),
        P("dp", "fsdp"),
        P("dp", "fsdp"),
        P(("dp", "fsdp")),
        P("dp", "fsdp"),
        P("fsdp", "dp"),
        P(("dp", "fsdp")),
        P(("dp", "fsdp")),
        P(),
        P(("dp", "fsdp"), None, None),
    )
    return jax.shard_map(
        partial(local, mesh.shape["dp"], mesh.shape["fsdp"]),
        mesh=mesh,
        in_specs=placed,
        out_specs=(
            P(("dp", "fsdp"), None, None),
            P(("dp", "fsdp"), None, None),
            P(("dp", "fsdp"), None, None),
            P("dp", "fsdp"),
            P("dp", "fsdp"),
            P("dp", "fsdp"),
            P(("dp", "fsdp")),
            P("dp", "fsdp"),
            P("fsdp", "dp"),
        ),
        check_vma=False,
    )
```

time: 854 us -> 369 us (0.43)
  waiting for transfers between devices: 472 us -> 104 us
  Pallas kernels: 0 us -> 154 us
  matrix products: 122 us -> 0 us
  blocking collectives: 121 us -> 0 us
  starting transfers between devices: 0.75 us -> 72.8 us
  local copies, waits for them, and re-layouts: 87.1 us -> 16.5 us
  between operations: 17.4 us -> 1.3 us
  other arithmetic: 29 us -> 19.3 us
    reduce_scatter x5 -> x0, waiting for transfers between devices: 232 us -> none  [the longest x1 96.3 us: local(): lax.psum_scatter(grad_down.astype(jnp.bfloat16), 'dp', scatter_dimension=...]
    pallas_call x0 -> x8, Pallas kernels: none -> 154 us  [call(): pl.pallas_call(body, name=name, out_shape=[jax.ShapeDtypeStruct(v.shape,...]
    unnamed x17 -> x0, waiting for transfers between devices: 144 us -> none
    dot_general x18 -> x0, matrix products: 122 us -> none  [the longest x1 28.5 us: local(): jnp.dot(first_norm, w_up, preferred_element_type=jnp.float32)]
    ppermute x0 -> x62, waiting for transfers between devices: none -> 104 us  [move(): return lax.ppermute(value, ('dp', 'fsdp'), self.pairs(step))]
    all_gather x4 -> x0, waiting for transfers between devices: 95.4 us -> none  [the longest x1 52.6 us: local(): lax.all_gather(down_part, 'dp', axis=0, tiled=True)]
    all_gather x7 -> x0, blocking collectives: 88.6 us -> none  [the longest x1 26.8 us: local(): lax.all_gather(vec_part, 'dp', axis=1, tiled=True)]
    ppermute x0 -> x62, starting transfers between devices: none -> 72.8 us  [move(): return lax.ppermute(value, ('dp', 'fsdp'), self.pairs(step))]
  transfers between devices with their start and end apart: 13 -> 62, of which waited for: 10 -> 22; matrix products, arithmetic and copies ran while one was open for 21% -> 8% of each run, Pallas kernels for 0% -> 36%
where the time goes in v1:
time: 369 us; the launch traced here: 368 us
  Pallas kernels  154 us (42%)
  waiting for transfers between devices  104 us (28%)
  starting transfers between devices  72.8 us (20%)
  other arithmetic  19.3 us (5%)
  local copies, waits for them, and re-layouts  16.5 us (4%)
    pallas_call x8, Pallas kernels, call(): pl.pallas_call(body, name=name, out_shape=[jax.ShapeDtypeStruct(v.shape,...  154 us
    ppermute x62, waiting for transfers between devices, move(): return lax.ppermute(value, ('dp', 'fsdp'), self.pairs(step))  104 us
    ppermute x62, starting transfers between devices, move(): return lax.ppermute(value, ('dp', 'fsdp'), self.pairs(step))  72.8 us
  transfers between devices with their start and end apart: 62, of which 22 were waited for; matrix products, arithmetic and copies ran while one was open for 8% of the time, Pallas kernels for 36%

profile of v1, /device:TPU:0, one launch (start us, length us, event | category | flops | bytes accessed | tf_op | source)
XLA Modules:
  0.0 368.0 jit_solution(2982592200351878761)
XLA Ops:
  6.1 3.1 collective-permute-start.2
  11.9 2.8 collective-permute-start.15
  14.8 4.6 %collective-permute-done.13 = bf16[48,1536]{1,0:T(8,128)(2,1)S(1)} collective-permute-done((bf16[48,1536]{1,0:T(8,128)(2,1)S(1)}, bf16[48,1536]{1,0:T(8,128)(2,1)S(1)}, u32[]{:S(2)}, u32[]{:S(2)}) %collective-permute-start.13) | collective-permute-done | bytes 147488 | tf_op jit(solution)/shard_map/ppermute | solution.py:37
  19.4 8.9 %collective-permute-start.3 = (bf16[48,1664]{1,0:T(8,128)(2,1)S(1)}, bf16[48,1664]{1,0:T(8,128)(2,1)S(1)}, u32[]{:S(2)}, u32[]{:S(2)}) collective-permute-start(bf16[48,1664]{1,0:T(8,128)(2,1)S(1)} %get-tuple-element.96), channel_id=1, source_target_pairs={{0,16},{1,17},{2,18},{3,19},{4,20},{5,21},{6,22},{7,23},{8,24},{9,... | collective-permute-start | bytes 479240 | tf_op jit(solution)/shard_map/ppermute | solution.py:37
  28.3 4.1 %collective-permute-start.4 = (bf16[48,1664]{1,0:T(8,128)(2,1)S(1)}, bf16[48,1664]{1,0:T(8,128)(2,1)S(1)}, u32[]{:S(2)}, u32[]{:S(2)}) collective-permute-start(bf16[48,1664]{1,0:T(8,128)(2,1)S(1)} %get-tuple-element.96), channel_id=1, source_target_pairs={{0,24},{1,25},{2,26},{3,27},{4,28},{5,29},{6,30},{7,31},{8,0},{9,1... | collective-permute-start | bytes 479240 | tf_op jit(solution)/shard_map/ppermute | solution.py:37
  38.2 2.7 collective-permute-start.24
  43.5 3.2 collective-permute-done.24
  46.7 1.7 collective-permute-start.5
  48.4 3.2 collective-permute-done.25
  55.6 14.3 %collective-permute-done.16.refs_1_.refs_7_ = bf16[4,48,1536]{2,1,0:T(8,128)(2,1)} collective-permute-done((bf16[4,48,1536]{2,1,0:T(8,128)(2,1)S(1)}, bf16[4,48,1536]{2,1,0:T(8,128)(2,1)}, u32[]{:S(2)}, u32[]{:S(2)}) %collective-permute-start.16) | collective-permute-done | bytes 589856 | tf_op jit(solution)/shard_map/ppermute | solution.py:37
  70.4 1.7 collective-permute-start.18
  72.1 4.4 %collective-permute-done.7.refs_3_.refs_11_.refs_17_ = bf16[4,48,1664]{2,1,0:T(8,128)(2,1)S(1)} collective-permute-done((bf16[4,48,1664]{2,1,0:T(8,128)(2,1)S(1)}, bf16[4,48,1664]{2,1,0:T(8,128)(2,1)S(1)}, u32[]{:S(2)}, u32[]{:S(2)}) %collective-permute-start.7) | collective-permute-done | bytes 639008 | tf_op jit(solution)/shard_map/ppermute | solution.py:37
  76.6 1.7 collective-permute-start.27
  78.3 4.7 %collective-permute-done.18.refs_3_.refs_9_ = bf16[4,48,1536]{2,1,0:T(8,128)(2,1)} collective-permute-done((bf16[4,48,1536]{2,1,0:T(8,128)(2,1)}, bf16[4,48,1536]{2,1,0:T(8,128)(2,1)}, u32[]{:S(2)}, u32[]{:S(2)}) %collective-permute-start.18) | collective-permute-done | bytes 589856 | tf_op jit(solution)/shard_map/ppermute | solution.py:37
  83.5 1.7 collective-permute-start.29
  86.7 2.2 small_values.1
  90.1 5.6 %collective-permute-done.29.refs_8_.refs_3_ = bf16[4,192,384]{2,1,0:T(8,128)(2,1)} collective-permute-done((bf16[4,192,384]{2,1,0:T(8,128)(2,1)}, bf16[4,192,384]{2,1,0:T(8,128)(2,1)}, u32[]{:S(2)}, u32[]{:S(2)}) %collective-permute-start.29) | collective-permute-done | bytes 589856 | tf_op jit(solution)/shard_map/ppermute | solution.py:37
  95.6 27.8 %attend.1 = (bf16[768,2304]{1,0:T(8,128)(2,1)}, bf16[768,768]{1,0:T(8,128)(2,1)}, bf16[768,768]{1,0:T(8,128)(2,1)}, f32[768,768]{1,0:T(8,128)}, f32[768,128]{1,0:T(8,128)}) custom-call(s32[4]{0:T(128)} %pad_add_fusion.where, s32[3]{0:T(128)} %lengths.5, bf16[768,768]{1,0:T(8,128)(2,1)} %bitcast.130, f32[8,768]{1,0:T(8,128)} %get-tuple-element.37.vec.refs_4_.refs_5_, ...), custom_call_target="tpu_custom_call" | custom-call | flops 4227858432 | bytes 20078620 | tf_op jit(solution)/shard_map/attend/pallas_call | solution.py:539
  123.4 17.8 %up.1 = (bf16[768,3072]{1,0:T(8,128)(2,1)}, bf16[768,3072]{1,0:T(8,128)(2,1)}) custom-call(s32[4]{0:T(128)} %pad_add_fusion.where, bf16[768,768]{1,0:T(8,128)(2,1)} %get-tuple-element.38.first_norm.refs_1_, f32[1,3072]{1,0:T(1,128)} %get-tuple-element.39.bias, bf16[4,48,1536]{2,1,0:T(8,128)(2,1)} %copy-done.8, ...), custom_call_target="tpu_custom_call" | custom-call | flops 3623878656 | bytes 15347728 | tf_op jit(solution)/shard_map/up/pallas_call | solution.py:539
  142.6 22.3 %down.1 = (bf16[768,768]{1,0:T(8,128)(2,1)}, f32[3,5,768]{2,1,0:T(8,128)}, f32[768,768]{1,0:T(8,128)}, bf16[768,768]{1,0:T(8,128)(2,1)}, f32[8,768]{1,0:T(8,128)...) custom-call(s32[4]{0:T(128)} %pad_add_fusion.where, s32[3]{0:T(128)} %lengths.5, s32[3]{0:T(128)} %depth.1, ...), custom_call_target="tpu_custom_call" | custom-call | flops 7247757312 | bytes 22508604 | tf_op jit(solution)/shard_map/down/pallas_call | solution.py:539
  165.6 26.8 %up_back.1 = (bf16[768,3072]{1,0:T(8,128)(2,1)}, f32[1,3072]{1,0:T(1,128)}, bf16[2,2,4,48,1536]{4,3,2,1,0:T(8,128)(2,1)}, bf16[2,2,4,48,1536]{4,3,2,1,0:T(8,128)(2,1)}) custom-call(s32[4]{0:T(128)} %pad_add_fusion.where, bf16[768,768]{1,0:T(8,128)(2,1)} %get-tuple-element.44.d_down, bf16[768,3072]{1,0:T(8,128)(2,1)} %get-tuple-element.45.slope, ...), custom_call_target="tpu_custom_call" | custom-call | flops 7247757312 | bytes 21245968 | tf_op jit(solution)/shard_map/up_back/pallas_call | solution.py:539
  192.4 15.2 %out_back.1 = (f32[768,768]{1,0:T(8,128)}, bf16[768,768]{1,0:T(8,128)(2,1)}, bf16[768,768]{1,0:T(8,128)(2,1)}, f32[8,768]{1,0:T(8,128)}) custom-call(s32[4]{0:T(128)} %pad_add_fusion.where, bf16[768,3072]{1,0:T(8,128)(2,1)} %get-tuple-element.46.refs_0_, f32[768,768]{1,0:T(8,128)} %get-tuple-element.47.refs_1_, f32[768,768]{1,0:T(8,128)} %get-tuple-element.48.refs_2_, ...), custom_call_target="tpu_custom_call" | custom-call | flops 5435817984 | bytes 25608208 | tf_op jit(solution)/shard_map/out_back/pallas_call | solution.py:539
  207.6 33.6 %attend_back.1 = (bf16[768,2304]{1,0:T(8,128)(2,1)}, f32[8,768]{1,0:T(8,128)}, bf16[2,2,4,48,1536]{4,3,2,1,0:T(8,128)(2,1)}, bf16[2,2,4,48,1536]{4,3,2,1,0:T(8,128)(2,1)}) custom-call(s32[4]{0:T(128)} %pad_add_fusion.where, s32[3]{0:T(128)} %lengths.5, bf16[768,2304]{1,0:T(8,128)(2,1)} %get-tuple-element.43.qkv, bf16[768,768]{1,0:T(8,128)(2,1)} %get-tuple-element.51.d_att, ...), custom_call_target="tpu_custom_call" | custom-call | flops 4227858432 | bytes 15360028 | tf_op jit(solution)/shard_map/attend_back/pallas_call | solution.py:539
  246.9 2.4 collective-permute-done.49
  249.4 4.0 %collective-permute-done.50 = f32[12,768]{1,0:T(8,128)S(1)} collective-permute-done((f32[12,768]{1,0:T(8,128)S(1)}, f32[12,768]{1,0:T(8,128)S(1)}, u32[]{:S(2)}, u32[]{:S(2)}) %collective-permute-start.50) | collective-permute-done | bytes 36896 | tf_op jit(solution)/shard_map/ppermute | solution.py:37
  253.4 1.7 collective-permute-start.51
  255.2 2.4 collective-permute-done.51
  257.6 4.1 %collective-permute-start.52 = (f32[12,768]{1,0:T(8,128)S(1)}, f32[12,768]{1,0:T(8,128)S(1)}, u32[]{:S(2)}, u32[]{:S(2)}) collective-permute-start(f32[12,768]{1,0:T(8,128)S(1)} %add.289), channel_id=1, source_target_pairs={{0,8},{1,9},{2,10},{3,11},{4,12},{5,13},{6,14},{7,15},{8,16},{9,17... | collective-permute-start | bytes 110600 | tf_op jit(solution)/shard_map/ppermute | solution.py:37
  261.7 2.0 collective-permute-start.53
  263.7 2.8 collective-permute-start.54
  266.5 2.7 fusion.2
  269.3 2.0 collective-permute-start.56
  271.3 2.8 fusion
  275.7 2.1 collective-permute-start.43
  277.8 8.8 %inputs.1 = bf16[768,768]{1,0:T(8,128)(2,1)} custom-call(s32[4]{0:T(128)} %pad_add_fusion.where, bf16[768,2304]{1,0:T(8,128)(2,1)} %get-tuple-element.53.d_qkv, f32[768,768]{1,0:T(8,128)} %get-tuple-element.54.d_resid, bf16[4,48,1664]{2,1,0:T(8,128)(2,1)} %copy-done, bf16[4,48,1664]{2,1,0:T(8,128)(2,1)} %copy-done.2, bf16[4,48,1664]{2,1,0:T(8,128)(2,1)} %copy-done.1, ...), custom_call_target="tpu_custom_call" | custom-call | flops 2717908992 | bytes 12189712 | tf_op jit(solution)/shard_map/inputs/pallas_call | solution.py:539
  291.1 2.5 fusion.3
  293.7 12.0 %collective-permute-done.35 = bf16[2,4,48,1536]{3,2,1,0:T(8,128)(2,1)} collective-permute-done((bf16[2,4,48,1536]{3,2,1,0:T(8,128)(2,1)}, bf16[2,4,48,1536]{3,2,1,0:T(8,128)(2,1)}, u32[]{:S(2)}, u32[]{:S(2)}) %collective-permute-start.35) | collective-permute-done | bytes 1179680 | tf_op jit(solution)/shard_map/ppermute | solution.py:37
  305.7 2.0 fusion.5
  307.8 19.2 %collective-permute-done.43 = bf16[2,4,48,1536]{3,2,1,0:T(8,128)(2,1)} collective-permute-done((bf16[2,4,48,1536]{3,2,1,0:T(8,128)(2,1)S(1)}, bf16[2,4,48,1536]{3,2,1,0:T(8,128)(2,1)}, u32[]{:S(2)}, u32[]{:S(2)}) %collective-permute-start.43) | collective-permute-done | bytes 1179680 | tf_op jit(solution)/shard_map/ppermute | solution.py:37
  327.0 2.0 fusion.4
  329.4 4.3 %collective-permute-start.37 = (bf16[48,1536]{1,0:T(8,128)(2,1)S(1)}, bf16[48,1536]{1,0:T(8,128)(2,1)S(1)}, u32[]{:S(2)}, u32[]{:S(2)}) collective-permute-start(bf16[48,1536]{1,0:T(8,128)(2,1)S(1)} %get-tuple-element.86), channel_id=1, source_target_pairs={{0,8},{1,9},{2,10},{3,11},{4,12},{5,13},{6,14},{7,15},{8,16},{9,17... | collective-permute-start | bytes 442376 | tf_op jit(solution)/shard_map/ppermute | solution.py:37
  333.8 5.2 %collective-permute-done.44 = bf16[4,48,1536]{2,1,0:T(8,128)(2,1)S(1)} collective-permute-done((bf16[4,48,1536]{2,1,0:T(8,128)(2,1)S(1)}, bf16[4,48,1536]{2,1,0:T(8,128)(2,1)S(1)}, u32[]{:S(2)}, u32[]{:S(2)}) %collective-permute-start.44) | collective-permute-done | bytes 589856 | tf_op jit(solution)/shard_map/ppermute | solution.py:37
  339.1 3.5 collective-permute-done.37
  344.0 5.6 %collective-permute-done.38 = bf16[48,1536]{1,0:T(8,128)(2,1)S(1)} collective-permute-done((bf16[48,1536]{1,0:T(8,128)(2,1)S(1)}, bf16[48,1536]{1,0:T(8,128)(2,1)S(1)}, u32[]{:S(2)}, u32[]{:S(2)}) %collective-permute-start.38) | collective-permute-done | bytes 147488 | tf_op jit(solution)/shard_map/ppermute | solution.py:37
  349.6 3.4 collective-permute-start.45
  353.0 3.4 collective-permute-start.46
  357.2 2.4 collective-permute-done.45
  359.6 3.2 collective-permute-done.46
  (193 shorter events, 46.1 us)
Async XLA Ops:
  5.6 32.5 %collective-permute-start.23 = (bf16[192,192]{1,0:T(8,128)(2,1)S(1)}, bf16[192,192]{1,0:T(8,128)(2,1)S(1)}, u32[]{:S(2)}, u32[]{:S(2)}) collective-permute-start(bf16[192,192]{1,0:T(8,128)(2,1)S(1)} %copy.25), channel_id=1, source_target_pairs={{0,1},{1,0},{2,3},{3,2},{4,5},{5,4},{6,7},{7,6},{8,9},{9,8},{10,11... | collective-permute-start | bytes 221192 | tf_op jit(solution)/shard_map/ppermute | solution.py:37
  6.1 28.0 %collective-permute-start.2 = (bf16[48,1664]{1,0:T(8,128)(2,1)S(1)}, bf16[48,1664]{1,0:T(8,128)(2,1)S(1)}, u32[]{:S(2)}, u32[]{:S(2)}) collective-permute-start(bf16[48,1664]{1,0:T(8,128)(2,1)S(1)} %get-tuple-element.96), channel_id=1, source_target_pairs={{0,8},{1,9},{2,10},{3,11},{4,12},{5,13},{6,14},{7,15},{8,16},{9,17... | collective-permute-start | bytes 479240 | tf_op jit(solution)/shard_map/ppermute | solution.py:37
  9.2 10.2 %collective-permute-start.13 = (bf16[48,1536]{1,0:T(8,128)(2,1)S(1)}, bf16[48,1536]{1,0:T(8,128)(2,1)S(1)}, u32[]{:S(2)}, u32[]{:S(2)}) collective-permute-start(bf16[48,1536]{1,0:T(8,128)(2,1)S(1)} %maximum_select_fusion.4), channel_id=1, source_target_pairs={{0,8},{1,9},{2,10},{3,11},{4,12},{5,13},{6,14},{7,15},{8,16},{9,17... | collective-permute-start | bytes 442376 | tf_op jit(solution)/shard_map/ppermute | solution.py:37
  10.8 17.5 %collective-permute-start.14 = (bf16[48,1536]{1,0:T(8,128)(2,1)S(1)}, bf16[48,1536]{1,0:T(8,128)(2,1)S(1)}, u32[]{:S(2)}, u32[]{:S(2)}) collective-permute-start(bf16[48,1536]{1,0:T(8,128)(2,1)S(1)} %maximum_select_fusion.4), channel_id=1, source_target_pairs={{0,16},{1,17},{2,18},{3,19},{4,20},{5,21},{6,22},{7,23},{8,24},{9,... | collective-permute-start | bytes 442376 | tf_op jit(solution)/shard_map/ppermute | solution.py:37
  11.9 20.5 %collective-permute-start.15 = (bf16[48,1536]{1,0:T(8,128)(2,1)S(1)}, bf16[48,1536]{1,0:T(8,128)(2,1)S(1)}, u32[]{:S(2)}, u32[]{:S(2)}) collective-permute-start(bf16[48,1536]{1,0:T(8,128)(2,1)S(1)} %maximum_select_fusion.4), channel_id=1, source_target_pairs={{0,24},{1,25},{2,26},{3,27},{4,28},{5,29},{6,30},{7,31},{8,0},{9,1... | collective-permute-start | bytes 442376 | tf_op jit(solution)/shard_map/ppermute | solution.py:37
  19.4 15.8 %collective-permute-start.3 = (bf16[48,1664]{1,0:T(8,128)(2,1)S(1)}, bf16[48,1664]{1,0:T(8,128)(2,1)S(1)}, u32[]{:S(2)}, u32[]{:S(2)}) collective-permute-start(bf16[48,1664]{1,0:T(8,128)(2,1)S(1)} %get-tuple-element.96), channel_id=1, source_target_pairs={{0,16},{1,17},{2,18},{3,19},{4,20},{5,21},{6,22},{7,23},{8,24},{9,... | collective-permute-start | bytes 479240 | tf_op jit(solution)/shard_map/ppermute | solution.py:37
  32.5 20.8 %collective-permute-start.17 = (bf16[4,48,1536]{2,1,0:T(8,128)(2,1)S(1)}, bf16[4,48,1536]{2,1,0:T(8,128)(2,1)}, u32[]{:S(2)}, u32[]{:S(2)}) collective-permute-start(bf16[4,48,1536]{2,1,0:T(8,128)(2,1)S(1)} %pad_maximum_fusion.1.refs_0_.refs_6_), channel_id=1, source_target_pairs={{0,2},{1,5},{2,0},{3,7},{4,6},{5,1},{6,4},{7,3},{8,10},{9,13},{10,... | collective-permute-start | bytes 1769480 | tf_op jit(solution)/shard_map/ppermute | solution.py:37
  36.5 18.1 %collective-permute-start.6 = (bf16[4,48,1664]{2,1,0:T(8,128)(2,1)S(1)}, bf16[4,48,1664]{2,1,0:T(8,128)(2,1)S(1)}, u32[]{:S(2)}, u32[]{:S(2)}) collective-permute-start(bf16[4,48,1664]{2,1,0:T(8,128)(2,1)S(1)} %pad_maximum_fusion.refs_0_.refs_8_.refs_14_), channel_id=1, source_target_pairs={{0,2},{1,5},{2,0},{3,7},{4,6},{5,1},{6,4},{7,3},{8,10},{9,13},{10,... | collective-permute-start | bytes 1916936 | tf_op jit(solution)/shard_map/ppermute | solution.py:37
  38.2 8.5 %collective-permute-start.24 = (bf16[192,384]{1,0:T(8,128)(2,1)S(1)}, bf16[192,384]{1,0:T(8,128)(2,1)S(1)}, u32[]{:S(2)}, u32[]{:S(2)}) collective-permute-start(bf16[192,384]{1,0:T(8,128)(2,1)S(1)} %maximum_select_fusion.6), channel_id=1, source_target_pairs={{0,8},{1,9},{2,10},{3,11},{4,12},{5,13},{6,14},{7,15},{8,16},{9,17... | collective-permute-start | bytes 442376 | tf_op jit(solution)/shard_map/ppermute | solution.py:37
  40.9 10.7 %collective-permute-start.25 = (bf16[192,384]{1,0:T(8,128)(2,1)S(1)}, bf16[192,384]{1,0:T(8,128)(2,1)S(1)}, u32[]{:S(2)}, u32[]{:S(2)}) collective-permute-start(bf16[192,384]{1,0:T(8,128)(2,1)S(1)} %maximum_select_fusion.6), channel_id=1, source_target_pairs={{0,16},{1,17},{2,18},{3,19},{4,20},{5,21},{6,22},{7,23},{8,24},{9,... | collective-permute-start | bytes 442376 | tf_op jit(solution)/shard_map/ppermute | solution.py:37
  42.5 9.9 %collective-permute-start.26 = (bf16[192,384]{1,0:T(8,128)(2,1)S(1)}, bf16[192,384]{1,0:T(8,128)(2,1)S(1)}, u32[]{:S(2)}, u32[]{:S(2)}) collective-permute-start(bf16[192,384]{1,0:T(8,128)(2,1)S(1)} %maximum_select_fusion.6), channel_id=1, source_target_pairs={{0,24},{1,25},{2,26},{3,27},{4,28},{5,29},{6,30},{7,31},{8,0},{9,1... | collective-permute-start | bytes 442376 | tf_op jit(solution)/shard_map/ppermute | solution.py:37
  46.7 23.7 %collective-permute-start.5 = (bf16[4,48,1664]{2,1,0:T(8,128)(2,1)S(1)}, bf16[4,48,1664]{2,1,0:T(8,128)(2,1)S(1)}, u32[]{:S(2)}, u32[]{:S(2)}) collective-permute-start(bf16[4,48,1664]{2,1,0:T(8,128)(2,1)S(1)} %pad_maximum_fusion.refs_0_.refs_8_.refs_14_), channel_id=1, source_target_pairs={{0,4},{1,3},{2,6},{3,1},{4,0},{5,7},{6,2},{7,5},{8,12},{9,11},{10,... | collective-permute-start | bytes 1916936 | tf_op jit(solution)/shard_map/ppermute | solution.py:37
  51.6 18.2 %collective-permute-start.16 = (bf16[4,48,1536]{2,1,0:T(8,128)(2,1)S(1)}, bf16[4,48,1536]{2,1,0:T(8,128)(2,1)}, u32[]{:S(2)}, u32[]{:S(2)}) collective-permute-start(bf16[4,48,1536]{2,1,0:T(8,128)(2,1)S(1)} %pad_maximum_fusion.1.refs_0_.refs_6_), channel_id=1, source_target_pairs={{0,4},{1,3},{2,6},{3,1},{4,0},{5,7},{6,2},{7,5},{8,12},{9,11},{10,... | collective-permute-start | bytes 1769480 | tf_op jit(solution)/shard_map/ppermute | solution.py:37
  52.3 17.5 %collective-permute-start.19 = (bf16[4,48,1536]{2,1,0:T(8,128)(2,1)S(1)}, bf16[4,48,1536]{2,1,0:T(8,128)(2,1)S(1)}, u32[]{:S(2)}, u32[]{:S(2)}) collective-permute-start(bf16[4,48,1536]{2,1,0:T(8,128)(2,1)S(1)} %pad_maximum_fusion.1.refs_0_.refs_6_), channel_id=1, source_target_pairs={{0,1},{1,0},{2,3},{3,2},{4,5},{5,4},{6,7},{7,6},{8,9},{9,8},{10,11... | collective-permute-start | bytes 1769480 | tf_op jit(solution)/shard_map/ppermute | solution.py:37
  53.3 17.2 %collective-permute-start.28 = (bf16[4,192,384]{2,1,0:T(8,128)(2,1)}, bf16[4,192,384]{2,1,0:T(8,128)(2,1)}, u32[]{:S(2)}, u32[]{:S(2)}) collective-permute-start(bf16[4,192,384]{2,1,0:T(8,128)(2,1)} %pad_maximum_fusion.2.refs_5_.refs_0_), channel_id=1, source_target_pairs={{0,2},{1,5},{2,0},{3,7},{4,6},{5,1},{6,4},{7,3},{8,10},{9,13},{10,... | collective-permute-start | bytes 1769480 | tf_op jit(solution)/shard_map/ppermute | solution.py:37
  54.6 22.0 %collective-permute-start.7 = (bf16[4,48,1664]{2,1,0:T(8,128)(2,1)S(1)}, bf16[4,48,1664]{2,1,0:T(8,128)(2,1)S(1)}, u32[]{:S(2)}, u32[]{:S(2)}) collective-permute-start(bf16[4,48,1664]{2,1,0:T(8,128)(2,1)S(1)} %collective-permute-done.6.refs_2_.refs_10_.refs_16_), channel_id=1, source_target_pairs={{0,4},{1,3},{2,6},{3,1},{4,0},{5,7},{6,2},{7,5},{8,12},{9,11},{10,... | collective-permute-start | bytes 1916936 | tf_op jit(solution)/shard_map/ppermute | solution.py:37
  69.8 13.2 %collective-permute-start.10 = (bf16[4,48,1664]{2,1,0:T(8,128)(2,1)S(1)}, bf16[4,48,1664]{2,1,0:T(8,128)(2,1)S(1)}, u32[]{:S(2)}, u32[]{:S(2)}) collective-permute-start(bf16[4,48,1664]{2,1,0:T(8,128)(2,1)S(1)} %collective-permute-done.6.refs_2_.refs_10_.refs_16_), channel_id=1, source_target_pairs={{0,1},{1,0},{2,3},{3,2},{4,5},{5,4},{6,7},{7,6},{8,9},{9,8},{10,11... | collective-permute-start | bytes 1916936 | tf_op jit(solution)/shard_map/ppermute | solution.py:37
  70.3 13.2 %collective-permute-start.9 = (bf16[4,48,1664]{2,1,0:T(8,128)(2,1)S(1)}, bf16[4,48,1664]{2,1,0:T(8,128)(2,1)S(1)}, u32[]{:S(2)}, u32[]{:S(2)}) collective-permute-start(bf16[4,48,1664]{2,1,0:T(8,128)(2,1)S(1)} %collective-permute-done.5.refs_1_.refs_9_.refs_15_), channel_id=1, source_target_pairs={{0,1},{1,0},{2,3},{3,2},{4,5},{5,4},{6,7},{7,6},{8,9},{9,8},{10,11... | collective-permute-start | bytes 1916936 | tf_op jit(solution)/shard_map/ppermute | solution.py:37
  70.4 12.6 %collective-permute-start.18 = (bf16[4,48,1536]{2,1,0:T(8,128)(2,1)}, bf16[4,48,1536]{2,1,0:T(8,128)(2,1)}, u32[]{:S(2)}, u32[]{:S(2)}) collective-permute-start(bf16[4,48,1536]{2,1,0:T(8,128)(2,1)} %collective-permute-done.17.refs_2_.refs_8_), channel_id=1, source_target_pairs={{0,4},{1,3},{2,6},{3,1},{4,0},{5,7},{6,2},{7,5},{8,12},{9,11},{10,... | collective-permute-start | bytes 1769480 | tf_op jit(solution)/shard_map/ppermute | solution.py:37
  76.6 8.6 %collective-permute-start.11 = (bf16[4,48,1664]{2,1,0:T(8,128)(2,1)S(1)}, bf16[4,48,1664]{2,1,0:T(8,128)(2,1)S(1)}, u32[]{:S(2)}, u32[]{:S(2)}) collective-permute-start(bf16[4,48,1664]{2,1,0:T(8,128)(2,1)S(1)} %collective-permute-done.7.refs_3_.refs_11_.refs_17_), channel_id=1, source_target_pairs={{0,1},{1,0},{2,3},{3,2},{4,5},{5,4},{6,7},{7,6},{8,9},{9,8},{10,11... | collective-permute-start | bytes 1916936 | tf_op jit(solution)/shard_map/ppermute | solution.py:37
  76.6 12.7 %collective-permute-start.27 = (bf16[4,192,384]{2,1,0:T(8,128)(2,1)}, bf16[4,192,384]{2,1,0:T(8,128)(2,1)}, u32[]{:S(2)}, u32[]{:S(2)}) collective-permute-start(bf16[4,192,384]{2,1,0:T(8,128)(2,1)} %pad_maximum_fusion.2.refs_5_.refs_0_), channel_id=1, source_target_pairs={{0,4},{1,3},{2,6},{3,1},{4,0},{5,7},{6,2},{7,5},{8,12},{9,11},{10,... | collective-permute-start | bytes 1769480 | tf_op jit(solution)/shard_map/ppermute | solution.py:37
  83.5 12.1 %collective-permute-start.29 = (bf16[4,192,384]{2,1,0:T(8,128)(2,1)}, bf16[4,192,384]{2,1,0:T(8,128)(2,1)}, u32[]{:S(2)}, u32[]{:S(2)}) collective-permute-start(bf16[4,192,384]{2,1,0:T(8,128)(2,1)} %collective-permute-done.28.refs_7_.refs_2_), channel_id=1, source_target_pairs={{0,4},{1,3},{2,6},{3,1},{4,0},{5,7},{6,2},{7,5},{8,12},{9,11},{10,... | collective-permute-start | bytes 1769480 | tf_op jit(solution)/shard_map/ppermute | solution.py:37
  86.0 37.4 %collective-permute-start.22 = (bf16[4,48,1536]{2,1,0:T(8,128)(2,1)}, bf16[4,48,1536]{2,1,0:T(8,128)(2,1)}, u32[]{:S(2)}, u32[]{:S(2)}) collective-permute-start(bf16[4,48,1536]{2,1,0:T(8,128)(2,1)} %collective-permute-done.18.refs_3_.refs_9_), channel_id=1, source_target_pairs={{0,1},{1,0},{2,3},{3,2},{4,5},{5,4},{6,7},{7,6},{8,9},{9,8},{10,11... | collective-permute-start | bytes 1769480 | tf_op jit(solution)/shard_map/ppermute | solution.py:37
  89.3 51.9 %collective-permute-start.30 = (bf16[4,192,384]{2,1,0:T(8,128)(2,1)}, bf16[4,192,384]{2,1,0:T(8,128)(2,1)S(1)}, u32[]{:S(2)}, u32[]{:S(2)}) collective-permute-start(bf16[4,192,384]{2,1,0:T(8,128)(2,1)} %pad_maximum_fusion.2.refs_5_.refs_0_), channel_id=1, source_target_pairs={{0,1},{1,0},{2,3},{3,2},{4,5},{5,4},{6,7},{7,6},{8,9},{9,8},{10,11... | collective-permute-start | bytes 1769480 | tf_op jit(solution)/shard_map/ppermute | solution.py:37
  89.5 51.7 %collective-permute-start.32 = (bf16[4,192,384]{2,1,0:T(8,128)(2,1)}, bf16[4,192,384]{2,1,0:T(8,128)(2,1)S(1)}, u32[]{:S(2)}, u32[]{:S(2)}) collective-permute-start(bf16[4,192,384]{2,1,0:T(8,128)(2,1)} %collective-permute-done.28.refs_7_.refs_2_), channel_id=1, source_target_pairs={{0,1},{1,0},{2,3},{3,2},{4,5},{5,4},{6,7},{7,6},{8,9},{9,8},{10,11... | collective-permute-start | bytes 1769480 | tf_op jit(solution)/shard_map/ppermute | solution.py:37
  89.8 51.4 %collective-permute-start.31 = (bf16[4,192,384]{2,1,0:T(8,128)(2,1)}, bf16[4,192,384]{2,1,0:T(8,128)(2,1)S(1)}, u32[]{:S(2)}, u32[]{:S(2)}) collective-permute-start(bf16[4,192,384]{2,1,0:T(8,128)(2,1)} %collective-permute-done.27.refs_6_.refs_1_), channel_id=1, source_target_pairs={{0,1},{1,0},{2,3},{3,2},{4,5},{5,4},{6,7},{7,6},{8,9},{9,8},{10,11... | collective-permute-start | bytes 1769480 | tf_op jit(solution)/shard_map/ppermute | solution.py:37
  95.6 45.6 %collective-permute-start.33 = (bf16[4,192,384]{2,1,0:T(8,128)(2,1)}, bf16[4,192,384]{2,1,0:T(8,128)(2,1)S(1)}, u32[]{:S(2)}, u32[]{:S(2)}) collective-permute-start(bf16[4,192,384]{2,1,0:T(8,128)(2,1)} %collective-permute-done.29.refs_8_.refs_3_), channel_id=1, source_target_pairs={{0,1},{1,0},{2,3},{3,2},{4,5},{5,4},{6,7},{7,6},{8,9},{9,8},{10,11... | collective-permute-start | bytes 1769480 | tf_op jit(solution)/shard_map/ppermute | solution.py:37
  165.0 98.7 %collective-permute-start.55 = (bf16[2,2,4,192,384]{4,3,2,1,0:T(8,128)(2,1)}, bf16[2,2,4,192,384]{4,3,2,1,0:T(8,128)(2,1)}, u32[]{:S(2)}, u32[]{:S(2)}) collective-permute-start(bf16[2,2,4,192,384]{4,3,2,1,0:T(8,128)(2,1)} %get-tuple-element.64), channel_id=1, source_target_pairs={{0,1},{1,0},{2,3},{3,2},{4,5},{5,4},{6,7},{7,6},{8,9},{9,8},{10,11... | collective-permute-start | bytes 7077896 | tf_op jit(solution)/shard_map/ppermute | solution.py:37
  241.2 28.1 %collective-permute-start.34 = (bf16[2,2,4,48,1536]{4,3,2,1,0:T(8,128)(2,1)}, bf16[2,2,4,48,1536]{4,3,2,1,0:T(8,128)(2,1)}, u32[]{:S(2)}, u32[]{:S(2)}) collective-permute-start(bf16[2,2,4,48,1536]{4,3,2,1,0:T(8,128)(2,1)} %get-tuple-element.56), channel_id=1, source_target_pairs={{0,1},{1,0},{2,3},{3,2},{4,5},{5,4},{6,7},{7,6},{8,9},{9,8},{10,11... | collective-permute-start | bytes 7077896 | tf_op jit(solution)/shard_map/ppermute | solution.py:37
  241.3 32.8 %collective-permute-start.42 = (bf16[2,2,4,48,1536]{4,3,2,1,0:T(8,128)(2,1)}, bf16[2,2,4,48,1536]{4,3,2,1,0:T(8,128)(2,1)}, u32[]{:S(2)}, u32[]{:S(2)}) collective-permute-start(bf16[2,2,4,48,1536]{4,3,2,1,0:T(8,128)(2,1)} %get-tuple-element.58), channel_id=1, source_target_pairs={{0,1},{1,0},{2,3},{3,2},{4,5},{5,4},{6,7},{7,6},{8,9},{9,8},{10,11... | collective-permute-start | bytes 7077896 | tf_op jit(solution)/shard_map/ppermute | solution.py:37
  257.6 18.1 %collective-permute-start.52 = (f32[12,768]{1,0:T(8,128)S(1)}, f32[12,768]{1,0:T(8,128)S(1)}, u32[]{:S(2)}, u32[]{:S(2)}) collective-permute-start(f32[12,768]{1,0:T(8,128)S(1)} %add.289), channel_id=1, source_target_pairs={{0,8},{1,9},{2,10},{3,11},{4,12},{5,13},{6,14},{7,15},{8,16},{9,17... | collective-permute-start | bytes 110600 | tf_op jit(solution)/shard_map/ppermute | solution.py:37
  261.7 25.5 %collective-permute-start.53 = (f32[12,768]{1,0:T(8,128)S(1)}, f32[12,768]{1,0:T(8,128)S(1)}, u32[]{:S(2)}, u32[]{:S(2)}) collective-permute-start(f32[12,768]{1,0:T(8,128)S(1)} %add.289), channel_id=1, source_target_pairs={{0,16},{1,17},{2,18},{3,19},{4,20},{5,21},{6,22},{7,23},{8,24},{9,... | collective-permute-start | bytes 110600 | tf_op jit(solution)/shard_map/ppermute | solution.py:37
  263.7 23.5 %collective-permute-start.54 = (f32[12,768]{1,0:T(8,128)S(1)}, f32[12,768]{1,0:T(8,128)S(1)}, u32[]{:S(2)}, u32[]{:S(2)}) collective-permute-start(f32[12,768]{1,0:T(8,128)S(1)} %add.289), channel_id=1, source_target_pairs={{0,24},{1,25},{2,26},{3,27},{4,28},{5,29},{6,30},{7,31},{8,0},{9,1... | collective-permute-start | bytes 110600 | tf_op jit(solution)/shard_map/ppermute | solution.py:37
  269.3 21.8 %collective-permute-start.56 = (bf16[2,4,192,384]{3,2,1,0:T(8,128)(2,1)}, bf16[2,4,192,384]{3,2,1,0:T(8,128)(2,1)}, u32[]{:S(2)}, u32[]{:S(2)}) collective-permute-start(bf16[2,4,192,384]{3,2,1,0:T(8,128)(2,1)} %fusion.2), channel_id=1, source_target_pairs={{0,4},{1,3},{2,6},{3,1},{4,0},{5,7},{6,2},{7,5},{8,12},{9,11},{10,... | collective-permute-start | bytes 3538952 | tf_op jit(solution)/shard_map/ppermute | solution.py:37
  274.1 31.6 %collective-permute-start.35 = (bf16[2,4,48,1536]{3,2,1,0:T(8,128)(2,1)}, bf16[2,4,48,1536]{3,2,1,0:T(8,128)(2,1)}, u32[]{:S(2)}, u32[]{:S(2)}) collective-permute-start(bf16[2,4,48,1536]{3,2,1,0:T(8,128)(2,1)} %fusion), channel_id=1, source_target_pairs={{0,4},{1,3},{2,6},{3,1},{4,0},{5,7},{6,2},{7,5},{8,12},{9,11},{10,... | collective-permute-start | bytes 3538952 | tf_op jit(solution)/shard_map/ppermute | solution.py:37
  275.7 51.3 %collective-permute-start.43 = (bf16[2,4,48,1536]{3,2,1,0:T(8,128)(2,1)S(1)}, bf16[2,4,48,1536]{3,2,1,0:T(8,128)(2,1)}, u32[]{:S(2)}, u32[]{:S(2)}) collective-permute-start(bf16[2,4,48,1536]{3,2,1,0:T(8,128)(2,1)S(1)} %fusion.1), channel_id=1, source_target_pairs={{0,4},{1,3},{2,6},{3,1},{4,0},{5,7},{6,2},{7,5},{8,12},{9,11},{10,... | collective-permute-start | bytes 3538952 | tf_op jit(solution)/shard_map/ppermute | solution.py:37
  293.6 35.4 %collective-permute-start.57 = (bf16[4,192,384]{2,1,0:T(8,128)(2,1)S(1)}, bf16[4,192,384]{2,1,0:T(8,128)(2,1)S(1)}, u32[]{:S(2)}, u32[]{:S(2)}) collective-permute-start(bf16[4,192,384]{2,1,0:T(8,128)(2,1)S(1)} %get-tuple-element.74), channel_id=1, source_target_pairs={{0,2},{1,5},{2,0},{3,7},{4,6},{5,1},{6,4},{7,3},{8,10},{9,13},{10,... | collective-permute-start | bytes 1769480 | tf_op jit(solution)/shard_map/ppermute | solution.py:37
  307.7 21.6 %collective-permute-start.36 = (bf16[4,48,1536]{2,1,0:T(8,128)(2,1)S(1)}, bf16[4,48,1536]{2,1,0:T(8,128)(2,1)S(1)}, u32[]{:S(2)}, u32[]{:S(2)}) collective-permute-start(bf16[4,48,1536]{2,1,0:T(8,128)(2,1)S(1)} %get-tuple-element.78), channel_id=1, source_target_pairs={{0,2},{1,5},{2,0},{3,7},{4,6},{5,1},{6,4},{7,3},{8,10},{9,13},{10,... | collective-permute-start | bytes 1769480 | tf_op jit(solution)/shard_map/ppermute | solution.py:37
  329.0 9.9 %collective-permute-start.44 = (bf16[4,48,1536]{2,1,0:T(8,128)(2,1)S(1)}, bf16[4,48,1536]{2,1,0:T(8,128)(2,1)S(1)}, u32[]{:S(2)}, u32[]{:S(2)}) collective-permute-start(bf16[4,48,1536]{2,1,0:T(8,128)(2,1)S(1)} %get-tuple-element.76), channel_id=1, source_target_pairs={{0,2},{1,5},{2,0},{3,7},{4,6},{5,1},{6,4},{7,3},{8,10},{9,13},{10,... | collective-permute-start | bytes 1769480 | tf_op jit(solution)/shard_map/ppermute | solution.py:37
  329.2 27.3 %collective-permute-start.58 = (bf16[192,384]{1,0:T(8,128)(2,1)S(1)}, bf16[192,384]{1,0:T(8,128)(2,1)S(1)}, u32[]{:S(2)}, u32[]{:S(2)}) collective-permute-start(bf16[192,384]{1,0:T(8,128)(2,1)S(1)} %get-tuple-element.80), channel_id=1, source_target_pairs={{0,8},{1,9},{2,10},{3,11},{4,12},{5,13},{6,14},{7,15},{8,16},{9,17... | collective-permute-start | bytes 442376 | tf_op jit(solution)/shard_map/ppermute | solution.py:37
  329.2 27.3 %collective-permute-start.59 = (bf16[192,384]{1,0:T(8,128)(2,1)S(1)}, bf16[192,384]{1,0:T(8,128)(2,1)S(1)}, u32[]{:S(2)}, u32[]{:S(2)}) collective-permute-start(bf16[192,384]{1,0:T(8,128)(2,1)S(1)} %get-tuple-element.82), channel_id=1, source_target_pairs={{0,16},{1,17},{2,18},{3,19},{4,20},{5,21},{6,22},{7,23},{8,24},{9,... | collective-permute-start | bytes 442376 | tf_op jit(solution)/shard_map/ppermute | solution.py:37
  329.4 13.1 %collective-permute-start.37 = (bf16[48,1536]{1,0:T(8,128)(2,1)S(1)}, bf16[48,1536]{1,0:T(8,128)(2,1)S(1)}, u32[]{:S(2)}, u32[]{:S(2)}) collective-permute-start(bf16[48,1536]{1,0:T(8,128)(2,1)S(1)} %get-tuple-element.86), channel_id=1, source_target_pairs={{0,8},{1,9},{2,10},{3,11},{4,12},{5,13},{6,14},{7,15},{8,16},{9,17... | collective-permute-start | bytes 442376 | tf_op jit(solution)/shard_map/ppermute | solution.py:37
  333.8 15.8 %collective-permute-start.38 = (bf16[48,1536]{1,0:T(8,128)(2,1)S(1)}, bf16[48,1536]{1,0:T(8,128)(2,1)S(1)}, u32[]{:S(2)}, u32[]{:S(2)}) collective-permute-start(bf16[48,1536]{1,0:T(8,128)(2,1)S(1)} %get-tuple-element.88), channel_id=1, source_target_pairs={{0,16},{1,17},{2,18},{3,19},{4,20},{5,21},{6,22},{7,23},{8,24},{9,... | collective-permute-start | bytes 442376 | tf_op jit(solution)/shard_map/ppermute | solution.py:37
  338.9 14.1 %collective-permute-start.39 = (bf16[48,1536]{1,0:T(8,128)(2,1)S(1)}, bf16[48,1536]{1,0:T(8,128)(2,1)S(1)}, u32[]{:S(2)}, u32[]{:S(2)}) collective-permute-start(bf16[48,1536]{1,0:T(8,128)(2,1)S(1)} %get-tuple-element.87), channel_id=1, source_target_pairs={{0,24},{1,25},{2,26},{3,27},{4,28},{5,29},{6,30},{7,31},{8,0},{9,1... | collective-permute-start | bytes 442376 | tf_op jit(solution)/shard_map/ppermute | solution.py:37
  342.5 14.1 %collective-permute-start.60 = (bf16[192,384]{1,0:T(8,128)(2,1)S(1)}, bf16[192,384]{1,0:T(8,128)(2,1)S(1)}, u32[]{:S(2)}, u32[]{:S(2)}) collective-permute-start(bf16[192,384]{1,0:T(8,128)(2,1)S(1)} %get-tuple-element.81), channel_id=1, source_target_pairs={{0,24},{1,25},{2,26},{3,27},{4,28},{5,29},{6,30},{7,31},{8,0},{9,1... | collective-permute-start | bytes 442376 | tf_op jit(solution)/shard_map/ppermute | solution.py:37
  349.6 10.0 %collective-permute-start.45 = (bf16[48,1536]{1,0:T(8,128)(2,1)S(1)}, bf16[48,1536]{1,0:T(8,128)(2,1)S(1)}, u32[]{:S(2)}, u32[]{:S(2)}) collective-permute-start(bf16[48,1536]{1,0:T(8,128)(2,1)S(1)} %get-tuple-element.83), channel_id=1, source_target_pairs={{0,8},{1,9},{2,10},{3,11},{4,12},{5,13},{6,14},{7,15},{8,16},{9,17... | collective-permute-start | bytes 442376 | tf_op jit(solution)/shard_map/ppermute | solution.py:37
  353.0 9.8 %collective-permute-start.46 = (bf16[48,1536]{1,0:T(8,128)(2,1)S(1)}, bf16[48,1536]{1,0:T(8,128)(2,1)S(1)}, u32[]{:S(2)}, u32[]{:S(2)}) collective-permute-start(bf16[48,1536]{1,0:T(8,128)(2,1)S(1)} %get-tuple-element.85), channel_id=1, source_target_pairs={{0,16},{1,17},{2,18},{3,19},{4,20},{5,21},{6,22},{7,23},{8,24},{9,... | collective-permute-start | bytes 442376 | tf_op jit(solution)/shard_map/ppermute | solution.py:37
  357.2 9.1 %collective-permute-start.61 = (f32[192,192]{1,0:T(8,128)S(1)}, f32[192,192]{1,0:T(8,128)S(1)}, u32[]{:S(2)}, u32[]{:S(2)}) collective-permute-start(f32[192,192]{1,0:T(8,128)S(1)} %get-tuple-element.90), channel_id=1, source_target_pairs={{0,1},{1,0},{2,3},{3,2},{4,5},{5,4},{6,7},{7,6},{8,9},{9,8},{10,11... | collective-permute-start | bytes 442376 | tf_op jit(solution)/shard_map/ppermute | solution.py:37
  (40 other events, 382.2 us)
